TPU v7x, 512 devices: a whole 4x8x8 slice. The times are simulated.
512 devices in a mesh: seq: 32 (over y, x), head: 2 (over core), expert: 8 (over z).
Axes of the slice: x: 4, y: 8, z: 8, core: 2. Of those that a mesh axis runs over, the one named last changes fastest.
Arguments:
- query_proj: bfloat16 [8, 4096, 2048], P('expert', 'seq', 'head'), may hold values from -6 to 6
- key_proj: bfloat16 [8, 4096, 2048], P('expert', 'seq', 'head'), may hold values from -6 to 6
- value_proj: bfloat16 [8, 4096, 2048], P('expert', 'seq', 'head'), may hold values from -6 to 6
- init_state: float32 [8, 16, 128, 128], P('expert', 'head'), may hold values from -384 to 384
- residual: bfloat16 [8, 4096, 2048], P('expert', ('seq', 'head')), may hold values from -6 to 6
- out_gain: float32 [2048], P('head'), may hold values from 0.1 to 1.9
- proj_weight: bfloat16 [2048, 2048], P('head', 'expert'), may hold values from -0.125 to 0.125
- moe_gain: float32 [2048], replicated, may hold values from 0.1 to 1.9
- w_gate: bfloat16 [64, 704, 2048], P(('seq', 'head'), None, 'expert'), may hold values from -0.125 to 0.125
- w_up: bfloat16 [64, 704, 2048], P(('seq', 'head'), None, 'expert'), may hold values from -0.125 to 0.125
- w_down: bfloat16 [64, 704, 2048], P(('seq', 'head'), None, 'expert'), may hold values from -0.21875 to 0.21875
- expert_ids: int32 [8, 4096, 6], P('expert', ('seq', 'head')), may hold values from 0 to 63, all different within a row; in each aligned block of 64 rows (0 to 63, 64 to 127, ..., all dimensions but the last counted through in order) at most 8 rows name the same one
- gate_weights: float32 [8, 4096, 6], P('expert', ('seq', 'head')), may hold values from 0.05 to 0.5
Outputs:
- layer_out: bfloat16 [8, 4096, 2048], P('expert', ('seq', 'head'))
Inputs may be any that keep to these rules, and one draw needn't show every extreme that they name: `expert_ids`: each token names 6 different experts. Among the 64 tokens of one device (aligned blocks of 64 positions) no expert is named more than 8 times, a bound that some block reaches.
All inputs are finite; a program needn't handle non-finite values.
Results may differ from a plain program's by a relative error of at most 0.019.
Values may be sent and summed in bfloat16 or wider, within the bound.
A program may use at most 128 MiB of HBM per device.

v0:
```python
import jax
import jax.numpy as jnp
from jax import lax
from jax.sharding import PartitionSpec as P

D = 2048
HD = 128
TOP = 6


HIGHEST = lax.Precision.HIGHEST


def carried_in(x, axis, join, neutral):
    place = lax.axis_index(axis)
    gathered = lax.all_gather(x.astype(jnp.bfloat16), axis)
    state = jnp.zeros_like(x) + jnp.asarray(neutral, x.dtype)

    def one(turn, state):
        return join(state, lax.dynamic_index_in_dim(gathered, turn, 0, False).astype(x.dtype))

    return lax.fori_loop(0, place, one, state)


def add_states(earlier, later):
    return earlier + later


def shards(
    query_proj,
    key_proj,
    value_proj,
    init_state,
    residual,
    out_gain,
    proj_weight,
    moe_gain,
    w_gate,
    w_up,
    w_down,
    expert_ids,
    gate_weights,
):
    tok_count = query_proj.shape[1]
    feat_width = query_proj.shape[2]
    head_count = feat_width // HD

    def to_heads(matrix):
        return matrix[0].astype(jnp.float32).reshape(tok_count, head_count, HD).transpose(1, 0, 2)

    query_heads = to_heads(query_proj)
    key_heads = to_heads(key_proj)
    value_heads = to_heads(value_proj)
    local_state = jnp.einsum("hsd,hse->hde", key_heads, value_heads, precision=HIGHEST)
    scanned = carried_in(local_state, "seq", add_states, jnp.zeros_like(local_state))
    prior_state = init_state[0] + scanned
    causal = jnp.tril(jnp.ones((tok_count, tok_count), jnp.float32))
    scores = jnp.einsum("htd,hsd->hts", query_heads, key_heads, precision=HIGHEST) * causal
    attended = jnp.einsum("hts,hsd->htd", scores, value_heads, precision=HIGHEST)
    attended = attended + jnp.einsum("htd,hde->hte", query_heads, prior_state, precision=HIGHEST)
    inv_norm = lax.rsqrt(jnp.mean(attended * attended, axis=-1, keepdims=True) + 1e-05)
    mixed = (
        (attended * inv_norm).transpose(1, 0, 2).reshape(tok_count, feat_width) * out_gain
    ).astype(jnp.bfloat16)
    row_count = residual.shape[1]
    wo_full, gate_full, up_full, down_full = (
        lax.all_gather(proj_weight, "expert", axis=1, tiled=True),
        lax.all_gather(w_gate, "expert", axis=2, tiled=True),
        lax.all_gather(w_up, "expert", axis=2, tiled=True),
        lax.all_gather(w_down, "expert", axis=2, tiled=True),
    )
    projected = lax.psum_scatter(
        jnp.dot(mixed, wo_full, preferred_element_type=jnp.float32).astype(jnp.bfloat16),
        "head",
        scatter_dimension=0,
        tiled=True,
    ).astype(jnp.float32)
    stream = (residual[0].astype(jnp.float32) + projected).astype(jnp.bfloat16)
    stream_f = lax.optimization_barrier(stream).astype(jnp.float32)
    moe_in = (
        stream_f
        * lax.rsqrt(jnp.mean(stream_f * stream_f, axis=-1, keepdims=True) + 1e-06)
        * moe_gain
    ).astype(jnp.bfloat16)
    experts_all = w_gate.shape[0] * lax.axis_size(("seq", "head"))
    capacity = max(2, 4 * row_count * TOP // (3 * experts_all))
    chosen = expert_ids[0].reshape(-1)
    onehot = (chosen[:, None] == lax.broadcasted_iota(jnp.int32, (1, experts_all), 1)).astype(
        jnp.int32
    )
    position = jnp.sum((jnp.cumsum(onehot, axis=0) - 1) * onehot, axis=1)
    target = (chosen * capacity + position).reshape(row_count, TOP)
    slot_ids = lax.broadcasted_iota(jnp.int32, (experts_all * capacity, 1, 1), 0)
    placing = jnp.any(target[None, :, :] == slot_ids, axis=-1).astype(jnp.bfloat16)
    outgoing = jnp.dot(placing, moe_in, preferred_element_type=jnp.float32).astype(jnp.bfloat16)
    outgoing = outgoing.reshape(experts_all, capacity, D)
    incoming = lax.all_to_all(outgoing, ("seq", "head"), split_axis=0, concat_axis=1, tiled=True)
    gate_act = jnp.einsum("ehd,erd->ehr", gate_full, incoming, preferred_element_type=jnp.float32)
    up_act = jnp.einsum("ehd,erd->ehr", up_full, incoming, preferred_element_type=jnp.float32)
    hidden = (jax.nn.silu(gate_act) * up_act).astype(jnp.bfloat16)
    results = jnp.einsum(
        "ehr,ehd->erd", hidden, down_full, preferred_element_type=jnp.float32
    ).astype(jnp.bfloat16)
    returned = lax.all_to_all(results, ("seq", "head"), split_axis=1, concat_axis=0, tiled=True)
    gathered_rows = jnp.take(
        returned.reshape(experts_all * capacity, D), target.reshape(-1), axis=0
    )
    gathered_rows = gathered_rows.reshape(row_count, TOP, D)
    combined = jnp.sum(gate_weights[0][:, :, None] * gathered_rows.astype(jnp.float32), axis=1)
    return (stream_f + combined).astype(jnp.bfloat16)[None]


def solution(mesh):
    placed = (
        P("expert", "seq", "head"),
        P("expert", "seq", "head"),
        P("expert", "seq", "head"),
        P("expert", "head", None, None),
        P("expert", ("seq", "head"), None),
        P("head"),
        P("head", "expert"),
        P(),
        P(("seq", "head"), None, "expert"),
        P(("seq", "head"), None, "expert"),
        P(("seq", "head"), None, "expert"),
        P("expert", ("seq", "head"), None),
        P("expert", ("seq", "head"), None),
    )
    return jax.shard_map(
        shards,
        mesh=mesh,
        in_specs=placed,
        out_specs=P("expert", ("seq", "head"), None),
        check_vma=False,
    )
```

profile of v0, /device:TPU:1, one launch (start us, length us, event | category | flops | bytes accessed | tf_op | source)
XLA Modules:
  0.0 490.3 jit_solution(9989508836682642384)
XLA Ops:
  6.5 1.0 copy.95
  7.6 1.1 copy.88
  8.7 0.9 convolution_convert_fusion.3
  9.7 0.7 all-gather.7.cloned.1.call-update
  10.5 0.2 convolution_multiply_fusion
  10.8 108.3 %all-gather.15.cloned.1.call-done = bf16[256,128,128]{2,1,0:T(8,128)(2,1)} async-done(((bf16[8,128,128]{2,1,0:T(8,128)(2,1)}), bf16[256,128,128]{2,1,0:T(8,128)(2,1)}) %all-gather.15.cloned.1.call-update) | async-done | bytes 8388624 | tf_op jit(solution)/shard_map/all_gather | solution.py:16
  119.1 1.0 copy-done.1
  120.2 0.6 fusion.46
  120.8 0.7 fusion.44
  121.6 0.2 fusion.42
  121.8 60.7 %all-gather.7.cloned.1.call-done = bf16[1024,2048]{1,0:T(8,128)(2,1)} async-done(((bf16[1024,256]{1,0:T(8,128)(2,1)}), bf16[1024,2048]{1,0:T(8,128)(2,1)}) %all-gather.7.cloned.1.call-update) | async-done | bytes 4194320 | tf_op jit(solution)/shard_map/all_gather | solution.py:67
  182.5 3.8 convolution_convert_fusion.2
  186.3 0.5 all-gather.9.cloned.1.call-update
  186.9 0.5 all-gather.11.cloned.1.call-update
  187.5 0.5 all-gather.13.cloned.1.call-update
  188.1 0.1 eq.41
  188.2 0.1 reshape_squeeze.3
  188.4 0.9 reduce-window.6
  189.3 0.2 slice_reduce_fusion
  189.6 0.1 fusion.60
  189.7 0.1 reduce_sum.45
  189.9 0.2 fusion.35
  190.1 14.3 %reduce-scatter.2.cloned.1.call-done = bf16[64,2048]{1,0:T(8,128)(2,1)} async-done(((bf16[128,2048]{1,0:T(8,128)(2,1)}), bf16[64,2048]{1,0:T(8,128)(2,1)}) %reduce-scatter.2.cloned.1.call-update) | async-done | bytes 262160 | tf_op jit(solution)/shard_map/reduce_scatter | solution.py:72
  204.4 1.0 fusion.41
  205.4 0.2 fusion.37
  205.6 2.2 fusion.5
  207.7 8.9 %all-to-all-start = ((bf16[64,8,2048]{2,1,0:T(8,128)(2,1)}), bf16[64,8,2048]{2,1,0:T(8,128)(2,1)S(1)}, u32[]{:S(2)}, u32[]{:S(2)}) async-start(bf16[64,8,2048]{2,1,0:T(8,128)(2,1)} %fusion.5), calls=%async_computation.1 | async-start | bytes 4194304 | tf_op jit(solution)/shard_map/all_to_all | solution.py:97
  216.7 42.7 %all-gather.9.cloned.1.call-done = bf16[1,704,2048]{2,1,0:T(8,128)(2,1)} async-done(((bf16[1,704,256]{2,1,0:T(8,128)(2,1)}), bf16[1,704,2048]{2,1,0:T(8,128)(2,1)}) %all-gather.9.cloned.1.call-update) | async-done | bytes 2883600 | tf_op jit(solution)/shard_map/all_gather | solution.py:68
  259.4 7.0 %all-to-all-done = bf16[64,8,2048]{2,1,0:T(8,128)(2,1)S(1)} async-done(((bf16[64,8,2048]{2,1,0:T(8,128)(2,1)}), bf16[64,8,2048]{2,1,0:T(8,128)(2,1)S(1)}, u32[]{:S(2)}, u32[]{:S(2)}) %all-to-all-start) | async-done | bytes 2097184 | tf_op jit(solution)/shard_map/all_to_all | solution.py:97
  266.3 5.4 %fusion.11 = f32[704,512]{1,0:T(8,128)} fusion(bf16[1,704,2048]{2,1,0:T(8,128)(2,1)} %all-gather.9.cloned.1.call-done, bf16[64,8,2048]{2,1,0:T(8,128)(2,1)S(1)} %all-to-all-done), kind=kOutput, calls=%fused_computation.16 | convolution fusion | flops 1476395008 | bytes 6422528 | tf_op jit(solution)/shard_map/ehd,erd->ehr/dot_general | solution.py:98
  271.7 43.8 %all-gather.11.cloned.1.call-done = bf16[1,704,2048]{2,1,0:T(8,128)(2,1)} async-done(((bf16[1,704,256]{2,1,0:T(8,128)(2,1)}), bf16[1,704,2048]{2,1,0:T(8,128)(2,1)}) %all-gather.11.cloned.1.call-update) | async-done | bytes 2883600 | tf_op jit(solution)/shard_map/all_gather | solution.py:69
  315.5 56.4 %all-gather.13.cloned.1.call-done = bf16[1,704,2048]{2,1,0:T(8,128)(2,1)} async-done(((bf16[1,704,256]{2,1,0:T(8,128)(2,1)}), bf16[1,704,2048]{2,1,0:T(8,128)(2,1)}) %all-gather.13.cloned.1.call-update) | async-done | bytes 2883600 | tf_op jit(solution)/shard_map/all_gather | solution.py:70
  371.9 7.2 %fusion.6 = bf16[1,512,2048]{2,1,0:T(8,128)(2,1)S(1)} fusion(bf16[1,704,2048]{2,1,0:T(8,128)(2,1)} %all-gather.13.cloned.1.call-done, bf16[1,704,2048]{2,1,0:T(8,128)(2,1)} %all-gather.11.cloned.1.call-done, bf16[64,8,2048]{2,1,0:T(8,128)(2,1)} %copy-done, f32[704,512]{1,0:T(8,128)} %fusion.11), kind=kOutput, calls=%fused_computation.11 | convolution fusion | flops 2956001280 | bytes 11403264 | tf_op jit(solution)/shard_map/ehr,ehd->erd/dot_general | solution.py:101
  379.1 5.2 %copy.121 = bf16[1,512,2048]{2,0,1:T(2,128)(2,1)} copy(bf16[1,512,2048]{2,1,0:T(8,128)(2,1)S(1)} %fusion.6) | data formatting | bytes 4194304 | tf_op jit(solution)/shard_map/convert_element_type | solution.py:103
  384.3 0.5 broadcast.124
  384.8 13.2 %reduce.4 = bf16[512,2048]{1,0:T(8,128)(2,1)S(1)} reduce(bf16[512,1,2048]{2,1,0:T(2,128)(2,1)} %bitcast.140, bf16[]{:T(256)} %broadcast.124), dimensions={1}, to_apply=%bitcast.135.reduce_sub_computation | reduce | bytes 4194306
  397.9 3.3 reshape.176
  401.2 13.4 %all-to-all-start.1 = ((bf16[64,2,8192]{2,1,0:T(2,128)(2,1)}), bf16[64,2,8192]{2,1,0:T(2,128)(2,1)S(1)}, u32[]{:S(2)}, u32[]{:S(2)}) async-start(bf16[64,2,8192]{2,1,0:T(2,128)(2,1)} %reshape.176), calls=%async_computation.2 | async-start | bytes 4194304 | tf_op jit(solution)/shard_map/all_to_all | solution.py:104
  414.6 0.1 reduce_sum.44
  414.9 0.1 mul.112
  415.1 0.1 copy.81
  415.4 48.9 %all-to-all-done.1 = bf16[64,2,8192]{2,1,0:T(2,128)(2,1)S(1)} async-done(((bf16[64,2,8192]{2,1,0:T(2,128)(2,1)}), bf16[64,2,8192]{2,1,0:T(2,128)(2,1)S(1)}, u32[]{:S(2)}, u32[]{:S(2)}) %all-to-all-start.1) | async-done | bytes 2097184 | tf_op jit(solution)/shard_map/all_to_all | solution.py:104
  464.3 6.8 %reshape.177 = bf16[512,1,2048]{2,1,0:T(2,128)(2,1)} reshape(bf16[64,2,8192]{2,1,0:T(2,128)(2,1)S(1)} %all-to-all-done.1) | data formatting | bytes 4194304
  471.1 3.5 copy.120
  474.5 3.1 gather_fusion
  477.7 2.5 gather.7
  480.2 2.5 multiply_reduce_fusion
  482.7 0.8 fusion.47
  (41 shorter events, 1.0 us)
Async XLA Ops:
  6.5 3.9 copy-start.3
  6.5 112.5 %all-gather.15.cloned.1.call-start = ((), (), s32[]{:S(2)}) async-start(), calls=%async_computation.8 | async-start | bytes 8650752 | tf_op jit(solution)/shard_map/all_gather | solution.py:16
  9.7 172.8 %all-gather.7.cloned.1.call-start = ((), (), s32[]{:S(2)}) async-start(), calls=%async_computation.3 | async-start | bytes 4718592 | tf_op jit(solution)/shard_map/all_gather | solution.py:67
  10.4 194.0 %reduce-scatter.2.cloned.1.call-start = ((), (), s32[]{:S(2)}) async-start(), calls=%async_computation.4 | async-start | bytes 786432 | tf_op jit(solution)/shard_map/reduce_scatter | solution.py:72
  119.1 1.0 copy-start.1
  120.8 0.8 copy-start.6
  121.8 66.2 %copy-start.4 = (s32[1,64,6]{1,0,2:T(1,128)S(1)}, s32[1,64,6]{1,0,2:T(1,128)}, u32[]{:S(2)}) copy-start(s32[1,64,6]{1,0,2:T(1,128)} %param.26) | copy-start | bytes 4612
  186.2 18.2 %copy-start.2 = (bf16[1,64,2048]{2,1,0:T(8,128)(2,1)S(1)}, bf16[1,64,2048]{2,1,0:T(8,128)(2,1)}, u32[]{:S(2)}) copy-start(bf16[1,64,2048]{2,1,0:T(8,128)(2,1)} %param.19) | copy-start | bytes 786436
  186.2 19.4 %copy-start.5 = (f32[2048]{0:T(1024)S(1)}, f32[2048]{0:T(1024)}, u32[]{:S(2)}) copy-start(f32[2048]{0:T(1024)} %param.22) | copy-start | bytes 24580
  186.2 73.1 %all-gather.9.cloned.1.call-start = ((), (), s32[]{:S(2)}) async-start(), calls=%async_computation.5 | async-start | bytes 3244032 | tf_op jit(solution)/shard_map/all_gather | solution.py:68
  186.8 128.6 %all-gather.11.cloned.1.call-start = ((), (), s32[]{:S(2)}) async-start(), calls=%async_computation.6 | async-start | bytes 3244032 | tf_op jit(solution)/shard_map/all_gather | solution.py:69
  187.4 184.5 %all-gather.13.cloned.1.call-start = ((), (), s32[]{:S(2)}) async-start(), calls=%async_computation.7 | async-start | bytes 3244032 | tf_op jit(solution)/shard_map/all_gather | solution.py:70
  207.7 58.6 %all-to-all-start = ((bf16[64,8,2048]{2,1,0:T(8,128)(2,1)}), bf16[64,8,2048]{2,1,0:T(8,128)(2,1)S(1)}, u32[]{:S(2)}, u32[]{:S(2)}) async-start(bf16[64,8,2048]{2,1,0:T(8,128)(2,1)} %fusion.5), calls=%async_computation.1 | async-start | bytes 4194304 | tf_op jit(solution)/shard_map/all_to_all | solution.py:97
  266.3 5.4 %copy-start = (bf16[64,8,2048]{2,1,0:T(8,128)(2,1)}, bf16[64,8,2048]{2,1,0:T(8,128)(2,1)S(1)}, u32[]{:S(2)}) copy-start(bf16[64,8,2048]{2,1,0:T(8,128)(2,1)S(1)} %all-to-all-done) | copy-start | bytes 6291460
  401.2 14.0 %copy-start.7 = (f32[1,64,6]{1,0,2:T(1,128)S(1)}, f32[1,64,6]{1,0,2:T(1,128)}, u32[]{:S(2)}) copy-start(f32[1,64,6]{1,0,2:T(1,128)} %param.27) | copy-start | bytes 4612
  401.2 63.1 %all-to-all-start.1 = ((bf16[64,2,8192]{2,1,0:T(2,128)(2,1)}), bf16[64,2,8192]{2,1,0:T(2,128)(2,1)S(1)}, u32[]{:S(2)}, u32[]{:S(2)}) async-start(bf16[64,2,8192]{2,1,0:T(2,128)(2,1)} %reshape.176), calls=%async_computation.2 | async-start | bytes 4194304 | tf_op jit(solution)/shard_map/all_to_all | solution.py:104
Sparse Core Ops, SparseCore 0:
  10.5 108.5 all-gather.14
  121.1 61.3 all-gather.6
  186.4 17.9 reduce-scatter.1
  206.4 52.8 all-gather.8
  261.4 54.0 all-gather.10
  317.5 54.3 all-gather.12
where the time goes:
time: 492 us; the launch traced here: 490 us
  waiting for transfers between devices  384 us (78%)
  local copies, waits for them, and re-layouts  29.5 us (6%)
  starting transfers between devices  22.5 us (5%)
  matrix products  20.9 us (4%)
  other arithmetic  19.2 us (4%)
  between operations  13.7 us (3%)
    all_gather x1, waiting for transfers between devices, carried_in(): gathered = lax.all_gather(x.astype(jnp.bfloat16), axis)  108 us
    all_gather x1, waiting for transfers between devices, shards(): lax.all_gather(proj_weight, 'expert', axis=1, tiled=True)  60.7 us
    all_gather x1, waiting for transfers between devices, shards(): lax.all_gather(w_down, 'expert', axis=2, tiled=True)  56.4 us
    all_to_all x1, waiting for transfers between devices, shards(): lax.all_to_all(results, ('seq', 'head'), split_axis=1, concat_axis=0, til...  48.9 us
    all_gather x1, waiting for transfers between devices, shards(): lax.all_gather(w_up, 'expert', axis=2, tiled=True)  43.8 us
    all_gather x1, waiting for transfers between devices, shards(): lax.all_gather(w_gate, 'expert', axis=2, tiled=True)  42.7 us
    unnamed x23, local copies, waits for them, and re-layouts  16.2 us
    reduce_scatter x1, waiting for transfers between devices, shards(): lax.psum_scatter(jnp.dot(mixed, wo_full, preferred_element_type=jnp.float...  14.3 us
  transfers between devices with their start and end apart: 8, of which 8 were waited for; matrix products, arithmetic and copies ran while one was open for 3% of the time, Pallas kernels for 0%

commit v1 on v0

v1 whole, which is shorter than its diff:
```python
import functools

import jax
import jax.numpy as jnp
from jax import lax
from jax.experimental import pallas as pl
from jax.experimental.pallas import tpu as pltpu
from jax.sharding import PartitionSpec as P

D = 2048
HALF = 1024
HD = 128
TOP = 6
CAP = 8
BLK = 2 * CAP
MESH = pl.DeviceIdType.MESH
BF16 = jnp.bfloat16
F32 = jnp.float32
VMEM_LIMIT = 56 * 2**20


def grid_of(seq):
    nx = 4 if seq == 32 else 2
    return nx, seq // nx


def dot(a, b, dims=((1,), (0,))):
    return lax.dot_general(a, b, (dims, ((), ())), preferred_element_type=F32)


def rows(index, size):
    return pl.ds(pl.multiple_of(index * size, size), size)


def remote(src, dst, send, recv, target):
    return pltpu.make_async_remote_copy(
        src_ref=src, dst_ref=dst, send_sem=send, recv_sem=recv, device_id=target, device_id_type=MESH
    )


def attend_kernel(
    nx, ny, q_ref, k_ref, v_ref, init_ref, gain_ref, mixed_ref,
    loc, xin, tot, yin, pre, pin, att, x_send, x_recv, y_send, y_recv, p_send, p_recv,
):
    s, h, z = lax.axis_index("seq"), lax.axis_index("head"), lax.axis_index("expert")
    y, x = s // nx, lax.rem(s, nx)
    heads = q_ref.shape[1] // HD
    part = heads // nx

    def at_x(d):
        return (y * nx + lax.rem(x + d, nx), h, z)

    def at_y(d):
        return (lax.rem(y + d, ny) * nx + x, h, z)

    barrier = pltpu.get_barrier_semaphore()
    for d in range(1, nx):
        pl.semaphore_signal(barrier, inc=1, device_id=at_x(d), device_id_type=MESH)
    for d in range(1, ny):
        pl.semaphore_signal(barrier, inc=1, device_id=at_y(d), device_id_type=MESH)
    for i in range(heads):
        cols = slice(i * HD, (i + 1) * HD)
        loc[i // part, i % part] = dot(k_ref[:, cols], v_ref[:, cols], ((0,), (0,))).astype(BF16)
    pl.semaphore_wait(barrier, nx - 1 + ny - 1)

    first = [
        remote(loc.at[lax.rem(x + d, nx)], xin.at[d], x_send.at[d], x_recv.at[d], at_x(d))
        for d in range(1, nx)
    ]
    for copy in first:
        copy.start()
    xin[0] = loc[x]
    for copy in first:
        copy.wait_recv()
    tot[...] = sum(xin[d].astype(F32) for d in range(nx)).astype(BF16)
    second = [remote(tot, yin.at[d], y_send.at[d], y_recv.at[d], at_y(d)) for d in range(1, ny)]
    for copy in second:
        copy.start()

    tokens = q_ref.shape[0]
    causal = lax.broadcasted_iota(jnp.int32, (tokens, tokens), 0) >= lax.broadcasted_iota(
        jnp.int32, (tokens, tokens), 1
    )
    for i in range(heads):
        cols = slice(i * HD, (i + 1) * HD)
        scores = dot(q_ref[:, cols], k_ref[:, cols], ((1,), (1,)))
        scores = jnp.where(causal, scores, 0.0).astype(BF16)
        att[:, cols] = dot(scores, v_ref[:, cols])

    before = jnp.zeros(tot.shape, F32)
    for d in range(1, ny):
        second[d - 1].wait_recv()
        before = before + yin[d].astype(F32) * (d <= y).astype(F32)
    third = []
    for e in range(nx):
        target = lax.rem(x + e, nx)
        state = before
        for d in range(nx):
            source = lax.rem(x + nx - d, nx)
            state = state + xin[d].astype(F32) * (source < target).astype(F32)
        pre[e] = state.astype(BF16)
        if e:
            copy = remote(pre.at[e], pin.at[e], p_send.at[e], p_recv.at[e], at_x(e))
            copy.start()
            third.append(copy)
    pin[0] = pre[0]
    for e in range(nx):
        if e:
            third[e - 1].wait_recv()
        for j in range(part):
            head = lax.rem(x + nx - e, nx) * part + j
            cols = rows(head, HD)
            state = (init_ref[head] + pin[e, j].astype(F32)).astype(BF16)
            out = att[:, cols] + dot(q_ref[:, cols], state)
            inv = lax.rsqrt(jnp.mean(out * out, axis=1, keepdims=True) + 1e-05)
            mixed_ref[:, cols] = (out * inv * gain_ref[:, cols]).astype(BF16)
    for copy in first + second + third:
        copy.wait_send()


def place(ids_ref, gates_ref, placing, weighing):
    tokens = ids_ref.shape[0]
    slots = placing.shape[1]
    experts = slots // BLK
    expert = lax.broadcasted_iota(jnp.int32, (tokens, experts), 1)
    chosen = jnp.zeros((tokens, experts), F32)
    gates = jnp.zeros((tokens, experts), F32)
    for k in range(TOP):
        match = ids_ref[:, k : k + 1] == expert
        chosen = chosen + jnp.where(match, 1.0, 0.0)
        gates = gates + jnp.where(match, gates_ref[:, k : k + 1], 0.0)
    earlier = lax.broadcasted_iota(jnp.int32, (tokens, tokens), 1) < lax.broadcasted_iota(
        jnp.int32, (tokens, tokens), 0
    )
    earlier = jnp.where(earlier, 1.0, 0.0).astype(BF16)
    order = dot(earlier, chosen.astype(BF16))
    turn = (chosen * (order + 1.0)).astype(BF16)
    spread = lax.broadcasted_iota(jnp.int32, (experts, slots), 1) // BLK == lax.broadcasted_iota(
        jnp.int32, (experts, slots), 0
    )
    spread = jnp.where(spread, 1.0, 0.0).astype(BF16)
    turn = dot(turn, spread)
    gates = dot(gates.astype(BF16), spread)
    slot = lax.broadcasted_iota(jnp.int32, (tokens, slots), 1)
    place_in = lax.rem(slot, BLK)
    for half in range(2):
        wanted = (place_in - (half * CAP - 1)).astype(F32)
        hit = (turn == wanted) & (place_in // CAP == half)
        span = slice(half * tokens, (half + 1) * tokens)
        placing[span, :] = jnp.where(hit, 1.0, 0.0).astype(BF16)
        weighing[span, :] = jnp.where(hit, gates, 0.0).astype(BF16)


def dispatch_kernel(
    mixed_ref, wo_ref, res_ref, gain_ref, ids_ref, gates_ref, stream_ref, weigh_ref, incoming_ref,
    proj, snd, rcv, placing, feats, outgoing, h_sem, own_sem, send, recv,
):
    s, h, z = lax.axis_index("seq"), lax.axis_index("head"), lax.axis_index("expert")
    count = lax.axis_size("seq") * lax.axis_size("head")
    me = s * 2 + h
    tokens = res_ref.shape[0]

    def device(index):
        return (index // 2, lax.rem(index, 2), z)

    barrier = pltpu.get_barrier_semaphore()

    def greet(off, carry):
        pl.semaphore_signal(
            barrier, inc=1, device_id=device(lax.rem(me + off, count)), device_id_type=MESH
        )
        return carry

    lax.fori_loop(1, count, greet, 0)
    width = 512
    for c in range(D // width):
        cols = slice(c * width, (c + 1) * width)
        proj[:, cols] = dot(mixed_ref[...], wo_ref[:, cols])
    snd[...] = proj[rows(1 - h, tokens), :].astype(BF16)
    pl.semaphore_wait(barrier, count - 1)
    half = remote(snd, rcv, h_sem.at[0], h_sem.at[1], (s, 1 - h, z))
    half.start()
    place(ids_ref, gates_ref, placing, weigh_ref)
    half.wait_recv()
    stream = (
        res_ref[...].astype(F32) + (proj[rows(h, tokens), :] + rcv[...].astype(F32))
    ).astype(BF16)
    stream_ref[...] = stream
    stream_f = stream.astype(F32)
    inv = lax.rsqrt(jnp.mean(stream_f * stream_f, axis=1, keepdims=True) + 1e-06)
    moe_in = (stream_f * inv * gain_ref[...]).astype(BF16)
    feats[:tokens, :] = moe_in[:, :HALF]
    feats[tokens:, :] = moe_in[:, HALF:]
    tile = 256
    for c in range(outgoing.shape[0] // tile):
        span = slice(c * tile, (c + 1) * tile)
        outgoing[span, :] = dot(placing[:, span], feats[...], ((0,), (0,))).astype(BF16)

    def block(off):
        target = lax.rem(me + off, count)
        return remote(
            outgoing.at[rows(target, BLK), :], incoming_ref.at[rows(off, BLK), :],
            send.at[off], recv.at[off], device(target),
        )

    def begin(off, carry):
        block(off).start()
        return carry

    def finish(off, carry):
        block(off).wait()
        return carry

    lax.fori_loop(1, count, begin, 0)
    own = pltpu.make_async_copy(
        outgoing.at[rows(me, BLK), :], incoming_ref.at[pl.ds(0, BLK), :], own_sem
    )
    own.start()
    own.wait()
    half.wait_send()
    lax.fori_loop(1, count, finish, 0)


def expert_kernel(
    x_ref, w_ref, stream_ref, weigh_ref, out_ref, results, returned, own_sem, send, recv
):
    s, h, z = lax.axis_index("seq"), lax.axis_index("head"), lax.axis_index("expert")
    count = lax.axis_size("seq") * lax.axis_size("head")
    me = s * 2 + h
    tokens = stream_ref.shape[0]
    hidden_width = w_ref.shape[0] // 3

    def device(index):
        return (index // 2, lax.rem(index, 2), z)

    barrier = pltpu.get_barrier_semaphore()

    def greet(off, carry):
        pl.semaphore_signal(
            barrier, inc=1, device_id=device(lax.rem(me + off, count)), device_id_type=MESH
        )
        return carry

    lax.fori_loop(1, count, greet, 0)

    def block(off):
        return remote(
            results.at[rows(off, BLK), :], returned.at[rows(me, BLK), :],
            send.at[off], recv.at[off], device(lax.rem(me + count - off, count)),
        )

    def begin(off, carry):
        block(off).start()
        return carry

    group = count // 2
    for c in range(2):
        span = slice(c * group * BLK, (c + 1) * group * BLK)
        x = x_ref[span, :].astype(F32).reshape(group, BLK, HALF)
        low = x[:, :CAP].reshape(group * CAP, HALF).astype(BF16)
        high = x[:, CAP:].reshape(group * CAP, HALF).astype(BF16)
        acts = []
        for i in range(2):
            span_w = slice(i * hidden_width, (i + 1) * hidden_width)
            acts.append(
                dot(low, w_ref[span_w, :HALF], ((1,), (1,)))
                + dot(high, w_ref[span_w, HALF:], ((1,), (1,)))
            )
        gate, up = acts
        hidden = (gate / (1.0 + jnp.exp(-gate)) * up).astype(BF16)
        outs = [
            dot(hidden, w_ref[2 * hidden_width :, i * HALF : (i + 1) * HALF]).reshape(group, CAP, HALF)
            for i in range(2)
        ]
        results[span, :] = jnp.concatenate(outs, axis=1).reshape(group * BLK, HALF).astype(BF16)
        if c == 0:
            pl.semaphore_wait(barrier, count - 1)
        lax.fori_loop(max(1, c * group), (c + 1) * group, begin, 0)
    own = pltpu.make_async_copy(
        results.at[pl.ds(0, BLK), :], returned.at[rows(me, BLK), :], own_sem
    )
    own.start()
    own.wait()

    def finish(off, carry):
        source = lax.rem(me + off, count)
        block(off).wait_send()
        remote(
            results.at[rows(off, BLK), :], returned.at[rows(source, BLK), :],
            send.at[off], recv.at[off], device(source),
        ).wait_recv()
        return carry

    lax.fori_loop(1, count, finish, 0)
    combined = dot(weigh_ref[...], returned[...])
    for half in range(2):
        cols = slice(half * HALF, (half + 1) * HALF)
        span = slice(half * tokens, (half + 1) * tokens)
        out_ref[:, cols] = (stream_ref[:, cols].astype(F32) + combined[span, :]).astype(BF16)


def in_vmem(n):
    return [pl.BlockSpec(memory_space=pltpu.VMEM)] * n


def shards(
    nx, ny,
    query_proj, key_proj, value_proj, init_state, residual, out_gain, proj_weight, moe_gain,
    w_gate, w_up, w_down, expert_ids, gate_weights,
):
    tok, width = query_proj.shape[1:]
    heads = width // HD
    part = heads // nx
    token_rows = residual.shape[1]
    count = nx * ny * 2
    slots = count * BLK

    wo_full = lax.all_gather(proj_weight, "expert", axis=1, tiled=True)
    stacked = jnp.concatenate([w_gate[0], w_up[0], w_down[0]], axis=0)
    w_full = lax.all_gather(stacked, "expert", axis=1, tiled=True)

    state = (part, HD, HD)
    mixed = pl.pallas_call(
        functools.partial(attend_kernel, nx, ny),
        out_shape=jax.ShapeDtypeStruct((tok, width), BF16),
        in_specs=in_vmem(5),
        out_specs=pl.BlockSpec(memory_space=pltpu.VMEM),
        scratch_shapes=[
            pltpu.VMEM((nx, *state), BF16),
            pltpu.VMEM((nx, *state), BF16),
            pltpu.VMEM(state, BF16),
            pltpu.VMEM((ny, *state), BF16),
            pltpu.VMEM((nx, *state), BF16),
            pltpu.VMEM((nx, *state), BF16),
            pltpu.VMEM((tok, width), F32),
            pltpu.SemaphoreType.DMA((nx,)),
            pltpu.SemaphoreType.DMA((nx,)),
            pltpu.SemaphoreType.DMA((ny,)),
            pltpu.SemaphoreType.DMA((ny,)),
            pltpu.SemaphoreType.DMA((nx,)),
            pltpu.SemaphoreType.DMA((nx,)),
        ],
        compiler_params=pltpu.CompilerParams(
            collective_id=0, has_side_effects=True, vmem_limit_bytes=VMEM_LIMIT
        ),
        cost_estimate=pl.CostEstimate(flops=10**9, bytes_accessed=10**8, transcendentals=0),
        name="attend",
    )(query_proj[0], key_proj[0], value_proj[0], init_state[0], out_gain[None, :])

    stream, weighing, incoming = pl.pallas_call(
        dispatch_kernel,
        out_shape=[
            jax.ShapeDtypeStruct((token_rows, D), BF16),
            jax.ShapeDtypeStruct((2 * token_rows, slots), BF16),
            jax.ShapeDtypeStruct((slots, HALF), BF16),
        ],
        in_specs=in_vmem(6),
        out_specs=[*in_vmem(2), pl.BlockSpec(memory_space=pl.ANY)],
        scratch_shapes=[
            pltpu.VMEM((tok, D), F32),
            pltpu.VMEM((token_rows, D), BF16),
            pltpu.VMEM((token_rows, D), BF16),
            pltpu.VMEM((2 * token_rows, slots), BF16),
            pltpu.VMEM((2 * token_rows, HALF), BF16),
            pltpu.VMEM((slots, HALF), BF16),
            pltpu.SemaphoreType.DMA((2,)),
            pltpu.SemaphoreType.DMA,
            pltpu.SemaphoreType.DMA((count,)),
            pltpu.SemaphoreType.DMA((count,)),
        ],
        compiler_params=pltpu.CompilerParams(
            collective_id=1, has_side_effects=True, vmem_limit_bytes=VMEM_LIMIT
        ),
        cost_estimate=pl.CostEstimate(flops=10**9, bytes_accessed=2 * 10**8, transcendentals=0),
        name="dispatch",
    )(mixed, wo_full, residual[0], moe_gain[None, :], expert_ids[0], gate_weights[0])

    out = pl.pallas_call(
        expert_kernel,
        out_shape=jax.ShapeDtypeStruct((token_rows, D), BF16),
        in_specs=in_vmem(4),
        out_specs=pl.BlockSpec(memory_space=pltpu.VMEM),
        scratch_shapes=[
            pltpu.VMEM((slots, HALF), BF16),
            pltpu.VMEM((slots, HALF), BF16),
            pltpu.SemaphoreType.DMA,
            pltpu.SemaphoreType.DMA((count,)),
            pltpu.SemaphoreType.DMA((count,)),
        ],
        compiler_params=pltpu.CompilerParams(
            collective_id=2, has_side_effects=True, vmem_limit_bytes=VMEM_LIMIT
        ),
        cost_estimate=pl.CostEstimate(flops=5 * 10**9, bytes_accessed=2 * 10**8, transcendentals=0),
        name="experts",
    )(incoming, w_full, stream, weighing)
    return out[None]


def solution(mesh):
    placed = (
        P("expert", "seq", "head"),
        P("expert", "seq", "head"),
        P("expert", "seq", "head"),
        P("expert", "head", None, None),
        P("expert", ("seq", "head"), None),
        P("head"),
        P("head", "expert"),
        P(),
        P(("seq", "head"), None, "expert"),
        P(("seq", "head"), None, "expert"),
        P(("seq", "head"), None, "expert"),
        P("expert", ("seq", "head"), None),
        P("expert", ("seq", "head"), None),
    )
    nx, ny = grid_of(mesh.shape["seq"])
    return jax.shard_map(
        functools.partial(shards, nx, ny),
        mesh=mesh,
        in_specs=placed,
        out_specs=P("expert", ("seq", "head"), None),
        check_vma=False,
    )
```

time: 492 us -> 260 us (0.53)
  waiting for transfers between devices: 384 us -> 78 us
  Pallas kernels: 0 us -> 163 us
  local copies, waits for them, and re-layouts: 29.5 us -> 3.1 us
  starting transfers between devices: 22.5 us -> 0.04 us
  matrix products: 20.9 us -> 0 us
  other arithmetic: 19.2 us -> 2.3 us
    all_gather x5 -> x2, waiting for transfers between devices: 312 us -> 77.2 us  [the longest x1 41.2 us: shards(): w_full = lax.all_gather(stacked, 'expert', axis=1, tiled=True)]
    pallas_call x0 -> x3, Pallas kernels: none -> 163 us  [the longest x1 67.5 us: shards(): pl.pallas_call(expert_kernel, out_shape=jax.ShapeDtypeStruct((token_rows,...]
    all_to_all x2 -> x0, waiting for transfers between devices: 55.9 us -> none  [the longest x1 48.9 us: shards(): lax.all_to_all(results, ('seq', 'head'), split_axis=1, concat_axis=0, til...]
    all_to_all x2 -> x0, starting transfers between devices: 22.3 us -> none  [the longest x1 13.4 us: shards(): lax.all_to_all(results, ('seq', 'head'), split_axis=1, concat_axis=0, til...]
    dot_general x8 -> x0, matrix products: 20.9 us -> none  [the longest x1 7.18 us: shards(): jnp.einsum('ehr,ehd->erd', hidden, down_full, preferred_element_type=jnp....]
    reduce_scatter x1 -> x0, waiting for transfers between devices: 14.3 us -> none  [shards(): lax.psum_scatter(jnp.dot(mixed, wo_full, preferred_element_type=jnp.float...]
    unnamed x1 -> x0, other arithmetic: 13.2 us -> none
    unnamed x23 -> x7, local copies, waits for them, and re-layouts: 16.2 us -> 3.1 us
  transfers between devices with their start and end apart: 8 -> 2, of which waited for: 8 -> 2; matrix products, arithmetic and copies ran while one was open for 3% -> 1% of each run, Pallas kernels for 0% -> 37%
where the time goes in v1:
time: 260 us
  Pallas kernels  163 us (63%)
  waiting for transfers between devices  78 us (30%)
  between operations  13.4 us (5%)
  local copies, waits for them, and re-layouts  3.1 us (1%)
    pallas_call x1, Pallas kernels, shards(): pl.pallas_call(expert_kernel, out_shape=jax.ShapeDtypeStruct((token_rows,...  67.5 us
    pallas_call x1, Pallas kernels, shards(): pl.pallas_call(dispatch_kernel, out_shape=[jax.ShapeDtypeStruct((token_ro...  64.7 us
    all_gather x1, waiting for transfers between devices, shards(): w_full = lax.all_gather(stacked, 'expert', axis=1, tiled=True)  41.2 us
    all_gather x1, waiting for transfers between devices, shards(): wo_full = lax.all_gather(proj_weight, 'expert', axis=1, tiled=True)  36 us
    pallas_call x1, Pallas kernels, shards(): pl.pallas_call(functools.partial(attend_kernel, nx, ny), out_shape=jax.Sh...  31.2 us
  transfers between devices with their start and end apart: 2, of which 2 were waited for; matrix products, arithmetic and copies ran while one was open for 1% of the time, Pallas kernels for 37%

profile of v1, /device:TPU:1, one launch (start us, length us, event | category | flops | bytes accessed | tf_op | source)
XLA Modules:
  0.0 260.3 jit_solution(7627729428844110022)
XLA Ops:
  6.5 0.0 copy-start
  6.5 0.0 copy-start.1
  6.5 0.0 all-gather.3.cloned.1.call-start
  6.5 0.7 all-gather.3.cloned.1.call-update
  7.3 0.0 all-gather.5.cloned.1.call-start
  7.3 2.3 pad_maximum_fusion
  9.6 0.0 all-gather.5.cloned.1.call-update
  9.6 0.0 copy-done
  9.6 0.7 copy.14
  10.4 0.0 copy-done.1
  10.4 0.7 copy.15
  11.1 31.2 %attend.1.mixed_ref = bf16[128,1024]{1,0:T(8,128)(2,1)} custom-call(bf16[128,1024]{1,0:T(8,128)(2,1)} %bitcast.22, bf16[128,1024]{1,0:T(8,128)(2,1)} %bitcast.23, bf16[128,1024]{1,0:T(8,128)(2,1)} %bitcast.24, f32[8,128,128]{2,1,0:T(8,128)} %bitcast.21, f32[1,1024]{1,0:T(1,128)} %bitcast.25), custom_call_target="tpu_custom_call" | custom-call | flops 1000000000 | bytes 100000000 | tf_op jit(solution)/shard_map/attend/pallas_call | solution.py:323
  42.3 36.0 %all-gather.3.cloned.1.call-done.wo_ref = bf16[1024,2048]{1,0:T(8,128)(2,1)} async-done(((bf16[1024,256]{1,0:T(8,128)(2,1)}), bf16[1024,2048]{1,0:T(8,128)(2,1)}) %all-gather.3.cloned.1.call-update) | async-done | bytes 4194320 | tf_op jit(solution)/shard_map/all_gather | solution.py:318
  78.3 64.7 %dispatch.1 = (bf16[64,2048]{1,0:T(8,128)(2,1)}, bf16[128,1024]{1,0:T(8,128)(2,1)}, bf16[1024,1024]{1,0:T(8,128)(2,1)}) custom-call(bf16[128,1024]{1,0:T(8,128)(2,1)} %attend.1.mixed_ref, bf16[1024,2048]{1,0:T(8,128)(2,1)} %all-gather.3.cloned.1.call-done.wo_ref, bf16[64,2048]{1,0:T(8,128)(2,1)} %bitcast.16, f32[1,2048]{1,0:T(1,128)} %bitcast.20, ...), custom_call_target="tpu_custom_call" | custom-call | flops 1000000000 | bytes 200000000 | tf_op jit(solution)/shard_map/dispatch/pallas_call | solution.py:350
  143.0 41.2 %all-gather.5.cloned.1.call-done.w_ref = bf16[2112,2048]{1,0:T(8,128)(2,1)} async-done(((bf16[2112,256]{1,0:T(8,128)(2,1)}), bf16[2112,2048]{1,0:T(8,128)(2,1)}) %all-gather.5.cloned.1.call-update) | async-done | bytes 8650768 | tf_op jit(solution)/shard_map/all_gather | solution.py:320
  184.2 67.5 %experts.1 = bf16[64,2048]{1,0:T(8,128)(2,1)} custom-call(bf16[1024,1024]{1,0:T(8,128)(2,1)} %get-tuple-element.8.x_ref, bf16[2112,2048]{1,0:T(8,128)(2,1)} %all-gather.5.cloned.1.call-done.w_ref, bf16[64,2048]{1,0:T(8,128)(2,1)} %get-tuple-element.9.stream_ref, bf16[128,1024]{1,0:T(8,128)(2,1)} %get-tuple-element.10.weigh_ref), custom_call_target="tpu_custom_call" | custom-call | flops 5000000000 | bytes 200000000 | tf_op jit(solution)/shard_map/experts/pallas_call | solution.py:378
  251.7 1.7 copy.17
Async XLA Ops:
  6.5 3.1 %copy-start = (s32[1,64,6]{1,0,2:T(1,128)S(1)}, s32[1,64,6]{1,0,2:T(1,128)}, u32[]{:S(2)}) copy-start(s32[1,64,6]{1,0,2:T(1,128)} %param.24) | copy-start | bytes 4612
  6.5 3.8 %copy-start.1 = (f32[1,64,6]{1,0,2:T(1,128)S(1)}, f32[1,64,6]{1,0,2:T(1,128)}, u32[]{:S(2)}) copy-start(f32[1,64,6]{1,0,2:T(1,128)} %param.25) | copy-start | bytes 4612
  6.5 71.7 %all-gather.3.cloned.1.call-start = ((), (), s32[]{:S(2)}) async-start(), calls=%async_computation | async-start | bytes 4718592 | tf_op jit(solution)/shard_map/all_gather | solution.py:318
  7.3 176.9 %all-gather.5.cloned.1.call-start = ((), (), s32[]{:S(2)}) async-start(), calls=%async_computation.1 | async-start | bytes 9732096 | tf_op jit(solution)/shard_map/all_gather | solution.py:320
Sparse Core Ops, SparseCore 0:
  9.4 68.8 all-gather.2
  80.3 103.8 all-gather.4

commit v2 on v1

v2 whole, which is shorter than its diff:
```python
import functools

import jax
import jax.numpy as jnp
from jax import lax
from jax.experimental import pallas as pl
from jax.experimental.pallas import tpu as pltpu
from jax.sharding import PartitionSpec as P

D = 2048
HALF = 1024
HD = 128
TOP = 6
CAP = 8
BLK = 2 * CAP
MESH = pl.DeviceIdType.MESH
BF16 = jnp.bfloat16
F32 = jnp.float32
VMEM_LIMIT = 56 * 2**20


def grid_of(seq):
    nx = 4 if seq == 32 else 2
    return nx, seq // nx


def dot(a, b, dims=((1,), (0,))):
    return lax.dot_general(a, b, (dims, ((), ())), preferred_element_type=F32)


def rows(index, size):
    return pl.ds(pl.multiple_of(index * size, size), size)


def remote(src, dst, send, recv, target):
    return pltpu.make_async_remote_copy(
        src_ref=src, dst_ref=dst, send_sem=send, recv_sem=recv, device_id=target, device_id_type=MESH
    )


def place(ids_ref, gates_ref, placing, weighing):
    tokens = ids_ref.shape[0]
    slots = placing.shape[1]
    experts = slots // BLK
    expert = lax.broadcasted_iota(jnp.int32, (tokens, experts), 1)
    chosen = jnp.zeros((tokens, experts), F32)
    gates = jnp.zeros((tokens, experts), F32)
    for k in range(TOP):
        match = ids_ref[:, k : k + 1] == expert
        chosen = chosen + jnp.where(match, 1.0, 0.0)
        gates = gates + jnp.where(match, gates_ref[:, k : k + 1], 0.0)
    earlier = lax.broadcasted_iota(jnp.int32, (tokens, tokens), 1) < lax.broadcasted_iota(
        jnp.int32, (tokens, tokens), 0
    )
    earlier = jnp.where(earlier, 1.0, 0.0).astype(BF16)
    order = dot(earlier, chosen.astype(BF16))
    turn = (chosen * (order + 1.0)).astype(BF16)
    spread = lax.broadcasted_iota(jnp.int32, (experts, slots), 1) // BLK == lax.broadcasted_iota(
        jnp.int32, (experts, slots), 0
    )
    spread = jnp.where(spread, 1.0, 0.0).astype(BF16)
    turn = dot(turn, spread)
    gates = dot(gates.astype(BF16), spread)
    slot = lax.broadcasted_iota(jnp.int32, (tokens, slots), 1)
    place_in = lax.rem(slot, BLK)
    for half in range(2):
        wanted = (place_in - (half * CAP - 1)).astype(F32)
        hit = (turn == wanted) & (place_in // CAP == half)
        span = slice(half * tokens, (half + 1) * tokens)
        placing[span, :] = jnp.where(hit, 1.0, 0.0).astype(BF16)
        weighing[span, :] = jnp.where(hit, gates, 0.0).astype(BF16)


def front_kernel(
    nx, ny, nz, q_ref, k_ref, v_ref, init_ref, out_gain_ref, wo_ref, res_ref, gain_ref, ids_ref, gates_ref,
    stream_ref, weigh_ref, incoming_ref,
    loc, xin, tot, yin, pre, pin, att, mixed, wo, proj, snd, rcv, placing, feats, outgoing,
    x_send, x_recv, y_send, y_recv, p_send, p_recv, wz_send, wz_recv, wy_send, wy_recv,
    right_send, right_recv, left_send, left_recv, pass_send, pass_recv, h_sem, own_sem, send, recv,
):
    s, h, z = lax.axis_index("seq"), lax.axis_index("head"), lax.axis_index("expert")
    y, x = s // nx, lax.rem(s, nx)
    count = nx * ny * 2
    me = s * 2 + h
    heads = q_ref.shape[1] // HD
    part = heads // nx
    tokens = res_ref.shape[0]
    depth = wo_ref.shape[0] // (nx * ny)
    width = wo_ref.shape[1]

    def device(index):
        return (index // 2, lax.rem(index, 2), z)

    def at_x(d):
        return (y * nx + lax.rem(x + d, nx), h, z)

    def at_y(d):
        return (lax.rem(y + d, ny) * nx + x, h, z)

    def at_z(d):
        return (s, h, lax.rem(z + d, nz))

    barrier = pltpu.get_barrier_semaphore()
    for d in range(1, nz):
        pl.semaphore_signal(barrier, inc=1, device_id=at_z(d), device_id_type=MESH)

    def greet(off, carry):
        pl.semaphore_signal(
            barrier, inc=1, device_id=device(lax.rem(me + off, count)), device_id_type=MESH
        )
        return carry

    with jax.named_scope("greet"):
        lax.fori_loop(1, count, greet, 0)
    with jax.named_scope("states"):
        for i in range(heads):
            cols = slice(i * HD, (i + 1) * HD)
            loc[i // part, i % part] = dot(k_ref[:, cols], v_ref[:, cols], ((0,), (0,))).astype(BF16)
    with jax.named_scope("barrier"):
        pl.semaphore_wait(barrier, count - 1 + nz - 1)

    first = [
        remote(loc.at[lax.rem(x + d, nx)], xin.at[d], x_send.at[d], x_recv.at[d], at_x(d))
        for d in range(1, nx)
    ]
    for copy in first:
        copy.start()

    def strip(dx, dy):
        return pl.ds(
            pl.multiple_of((lax.rem(x + dx, nx) * ny + lax.rem(y + dy, ny)) * depth, depth), depth
        )

    mine = strip(0, 0)

    def fetch(d, owner):
        return remote(
            wo_ref.at[mine, :], wo.at[owner, mine, :], wz_send.at[d], wz_recv.at[d], at_z(d)
        )

    for d in range(1, nz):
        fetch(d, z).start()

    def along_y(b, step):
        block = wo.at[:, strip(0, ny - b), :]
        arrives = (b + step) % ny
        return remote(block, block, wy_send.at[arrives], wy_recv.at[arrives], at_y(step))

    def landed_y(b, step):
        block = wo.at[:, strip(0, ny - b), :]
        return remote(block, block, wy_send.at[b], wy_recv.at[b], at_y(step))

    def along_x(b, dx, sends, recvs, step):
        block = wo.at[:, strip(dx, ny - b), :]
        return remote(block, block, sends.at[b], recvs.at[b], at_x(step))

    reach = ny // 2
    to_right = [0, *range(reach + 1, ny)]

    def spread(b):
        along_x(b, 0, right_send, right_recv, 1).start()
        along_x(b, 0, left_send, left_recv, nx - 1).start()

    def relay_y(b):
        if b <= reach:
            landed_y(b, 1).wait_recv()
            if b < reach:
                along_y(b, 1).start()
        else:
            landed_y(b, ny - 1).wait_recv()
            if b > reach + 1:
                along_y(b, ny - 1).start()
        spread(b)

    def relay_x(b):
        if b in to_right:
            along_x(b, nx - 1, right_send, right_recv, 1).wait_recv()
            along_x(b, nx - 1, pass_send, pass_recv, 1).start()
        else:
            along_x(b, 1, left_send, left_recv, nx - 1).wait_recv()
            along_x(b, 1, pass_send, pass_recv, nx - 1).start()

    with jax.named_scope("states_x"):
        xin[0] = loc[x]
        for copy in first:
            copy.wait_recv()
    tot[...] = sum(xin[d].astype(F32) for d in range(nx)).astype(BF16)
    second = [remote(tot, yin.at[d], y_send.at[d], y_recv.at[d], at_y(d)) for d in range(1, ny)]
    for copy in second:
        copy.start()

    with jax.named_scope("fetched"):
        wo[z, mine, :] = wo_ref[mine, :]
        for d in range(1, nz):
            fetch(d, lax.rem(z + nz - d, nz)).wait_recv()
    along_y(0, 1).start()
    along_y(0, ny - 1).start()
    spread(0)

    with jax.named_scope("inner"):
        positions = q_ref.shape[0]
        causal = lax.broadcasted_iota(jnp.int32, (positions, positions), 0) >= lax.broadcasted_iota(
            jnp.int32, (positions, positions), 1
        )
        for i in range(heads):
            cols = slice(i * HD, (i + 1) * HD)
            scores = dot(q_ref[:, cols], k_ref[:, cols], ((1,), (1,)))
            scores = jnp.where(causal, scores, 0.0).astype(BF16)
            att[:, cols] = dot(scores, v_ref[:, cols])
    with jax.named_scope("placing"):
        place(ids_ref, gates_ref, placing, weigh_ref)
    with jax.named_scope("relay_1"):
        relay_y(1)
        relay_y(ny - 1)
        relay_x(0)

    before = jnp.zeros(tot.shape, F32)
    with jax.named_scope("states_y"):
        for d in range(1, ny):
            second[d - 1].wait_recv()
            before = before + yin[d].astype(F32) * (d <= y).astype(F32)
    third = []
    for e in range(nx):
        target = lax.rem(x + e, nx)
        state = before
        for d in range(nx):
            source = lax.rem(x + nx - d, nx)
            state = state + xin[d].astype(F32) * (source < target).astype(F32)
        pre[e] = state.astype(BF16)
        if e:
            copy = remote(pre.at[e], pin.at[e], p_send.at[e], p_recv.at[e], at_x(e))
            copy.start()
            third.append(copy)
    pin[0] = pre[0]
    with jax.named_scope("relay_2"):
        for step in range(2, reach):
            relay_y(step)
            relay_y(ny - step)
            relay_x(step - 1)
            relay_x(ny - step + 1)
        relay_y(reach)
        relay_x(reach - 1)
        relay_x(reach + 1)
    with jax.named_scope("mix"):
        for e in range(nx):
            if e:
                third[e - 1].wait_recv()
            for j in range(part):
                head = lax.rem(x + nx - e, nx) * part + j
                cols = rows(head, HD)
                state = (init_ref[head] + pin[e, j].astype(F32)).astype(BF16)
                out = att[:, cols] + dot(q_ref[:, cols], state)
                inv = lax.rsqrt(jnp.mean(out * out, axis=1, keepdims=True) + 1e-05)
                mixed[:, cols] = (out * inv * out_gain_ref[:, cols]).astype(BF16)
    with jax.named_scope("relay_3"):
        relay_x(reach)
        for b in range(ny):
            if b in to_right:
                along_x(b, 1, left_send, left_recv, nx - 1).wait_recv()
                along_x(b, 2, pass_send, pass_recv, 1).wait_recv()
            else:
                along_x(b, nx - 1, right_send, right_recv, 1).wait_recv()
                along_x(b, 2, pass_send, pass_recv, nx - 1).wait_recv()

    with jax.named_scope("project"):
        for c in range(nz):
            proj[:, c * width : (c + 1) * width] = dot(mixed[...], wo[c])
    snd[...] = proj[rows(1 - h, tokens), :].astype(BF16)
    half = remote(snd, rcv, h_sem.at[0], h_sem.at[1], (s, 1 - h, z))
    half.start()
    for copy in first + second + third:
        copy.wait_send()
    for d in range(1, nz):
        fetch(d, z).wait_send()
    for b in range(ny):
        along_x(b, 0, right_send, right_recv, 1).wait_send()
        along_x(b, 0, left_send, left_recv, nx - 1).wait_send()
        if b in to_right:
            along_x(b, nx - 1, pass_send, pass_recv, 1).wait_send()
        else:
            along_x(b, 1, pass_send, pass_recv, nx - 1).wait_send()
        if b and b <= reach:
            along_y(b - 1, 1).wait_send()
        elif b:
            along_y((b + 1) % ny, ny - 1).wait_send()
    with jax.named_scope("other_half"):
        half.wait_recv()
    stream = (
        res_ref[...].astype(F32) + (proj[rows(h, tokens), :] + rcv[...].astype(F32))
    ).astype(BF16)
    stream_ref[...] = stream
    stream_f = stream.astype(F32)
    inv = lax.rsqrt(jnp.mean(stream_f * stream_f, axis=1, keepdims=True) + 1e-06)
    moe_in = (stream_f * inv * gain_ref[...]).astype(BF16)
    feats[:tokens, :] = moe_in[:, :HALF]
    feats[tokens:, :] = moe_in[:, HALF:]
    with jax.named_scope("outgoing"):
        tile = 256
        for c in range(outgoing.shape[0] // tile):
            span = slice(c * tile, (c + 1) * tile)
            outgoing[span, :] = dot(placing[:, span], feats[...], ((0,), (0,))).astype(BF16)

    def block(off):
        target = lax.rem(me + off, count)
        return remote(
            outgoing.at[rows(target, BLK), :], incoming_ref.at[rows(off, BLK), :],
            send.at[off], recv.at[off], device(target),
        )

    def begin(off, carry):
        block(off).start()
        return carry

    def finish(off, carry):
        block(off).wait()
        return carry

    with jax.named_scope("begin"):
        lax.fori_loop(1, count, begin, 0)
    own = pltpu.make_async_copy(
        outgoing.at[rows(me, BLK), :], incoming_ref.at[pl.ds(0, BLK), :], own_sem
    )
    own.start()
    own.wait()
    half.wait_send()
    with jax.named_scope("arrivals"):
        lax.fori_loop(1, count, finish, 0)


def expert_kernel(
    x_ref, w_ref, stream_ref, weigh_ref, out_ref, results, returned, own_sem, send, recv
):
    s, h, z = lax.axis_index("seq"), lax.axis_index("head"), lax.axis_index("expert")
    count = lax.axis_size("seq") * lax.axis_size("head")
    me = s * 2 + h
    tokens = stream_ref.shape[0]
    hidden_width = w_ref.shape[0] // 3

    def device(index):
        return (index // 2, lax.rem(index, 2), z)

    barrier = pltpu.get_barrier_semaphore()

    def greet(off, carry):
        pl.semaphore_signal(
            barrier, inc=1, device_id=device(lax.rem(me + off, count)), device_id_type=MESH
        )
        return carry

    with jax.named_scope("greet"):
        lax.fori_loop(1, count, greet, 0)

    def block(off):
        return remote(
            results.at[rows(off, BLK), :], returned.at[rows(me, BLK), :],
            send.at[off], recv.at[off], device(lax.rem(me + count - off, count)),
        )

    def begin(off, carry):
        block(off).start()
        return carry

    with jax.named_scope("experts"):
        group = count // 2
        for c in range(2):
            span = slice(c * group * BLK, (c + 1) * group * BLK)
            x = x_ref[span, :].astype(F32).reshape(group, BLK, HALF)
            low = x[:, :CAP].reshape(group * CAP, HALF).astype(BF16)
            high = x[:, CAP:].reshape(group * CAP, HALF).astype(BF16)
            acts = []
            for i in range(2):
                span_w = slice(i * hidden_width, (i + 1) * hidden_width)
                acts.append(
                    dot(low, w_ref[span_w, :HALF], ((1,), (1,)))
                    + dot(high, w_ref[span_w, HALF:], ((1,), (1,)))
                )
            gate, up = acts
            hidden = (gate / (1.0 + jnp.exp(-gate)) * up).astype(BF16)
            outs = [
                dot(hidden, w_ref[2 * hidden_width :, i * HALF : (i + 1) * HALF]).reshape(group, CAP, HALF)
                for i in range(2)
            ]
            results[span, :] = jnp.concatenate(outs, axis=1).reshape(group * BLK, HALF).astype(BF16)
            if c == 0:
                pl.semaphore_wait(barrier, count - 1)
            lax.fori_loop(max(1, c * group), (c + 1) * group, begin, 0)
    own = pltpu.make_async_copy(
        results.at[pl.ds(0, BLK), :], returned.at[rows(me, BLK), :], own_sem
    )
    own.start()
    own.wait()

    def finish(off, carry):
        source = lax.rem(me + off, count)
        block(off).wait_send()
        remote(
            results.at[rows(off, BLK), :], returned.at[rows(source, BLK), :],
            send.at[off], recv.at[off], device(source),
        ).wait_recv()
        return carry

    with jax.named_scope("arrivals"):
        lax.fori_loop(1, count, finish, 0)
    with jax.named_scope("combine"):
        combined = dot(weigh_ref[...], returned[...])
        for half in range(2):
            cols = slice(half * HALF, (half + 1) * HALF)
            span = slice(half * tokens, (half + 1) * tokens)
            out_ref[:, cols] = (stream_ref[:, cols].astype(F32) + combined[span, :]).astype(BF16)


def in_vmem(n):
    return [pl.BlockSpec(memory_space=pltpu.VMEM)] * n


def shards(
    nx, ny,
    query_proj, key_proj, value_proj, init_state, residual, out_gain, proj_weight, moe_gain,
    w_gate, w_up, w_down, expert_ids, gate_weights,
):
    tok, width = query_proj.shape[1:]
    heads = width // HD
    part = heads // nx
    token_rows = residual.shape[1]
    count = nx * ny * 2
    slots = count * BLK

    stacked = jnp.concatenate([w_gate[0], w_up[0], w_down[0]], axis=0)
    w_full = lax.all_gather(stacked, "expert", axis=1, tiled=True)

    state = (part, HD, HD)
    nz = lax.axis_size("expert")
    depth, shard = proj_weight.shape
    dma = pltpu.SemaphoreType.DMA
    stream, weighing, incoming = pl.pallas_call(
        functools.partial(front_kernel, nx, ny, nz),
        out_shape=[
            jax.ShapeDtypeStruct((token_rows, D), BF16),
            jax.ShapeDtypeStruct((2 * token_rows, slots), BF16),
            jax.ShapeDtypeStruct((slots, HALF), BF16),
        ],
        in_specs=in_vmem(10),
        out_specs=[*in_vmem(2), pl.BlockSpec(memory_space=pl.ANY)],
        scratch_shapes=[
            pltpu.VMEM((nx, *state), BF16),
            pltpu.VMEM((nx, *state), BF16),
            pltpu.VMEM(state, BF16),
            pltpu.VMEM((ny, *state), BF16),
            pltpu.VMEM((nx, *state), BF16),
            pltpu.VMEM((nx, *state), BF16),
            pltpu.VMEM((tok, width), F32),
            pltpu.VMEM((tok, width), BF16),
            pltpu.VMEM((nz, depth, shard), BF16),
            pltpu.VMEM((tok, D), F32),
            pltpu.VMEM((token_rows, D), BF16),
            pltpu.VMEM((token_rows, D), BF16),
            pltpu.VMEM((2 * token_rows, slots), BF16),
            pltpu.VMEM((2 * token_rows, HALF), BF16),
            pltpu.VMEM((slots, HALF), BF16),
            *[dma((n,)) for n in (nx, nx, ny, ny, nx, nx, nz, nz, ny, ny, ny, ny, ny, ny, ny, ny, 2)],
            dma,
            dma((count,)),
            dma((count,)),
        ],
        compiler_params=pltpu.CompilerParams(
            collective_id=0, has_side_effects=True, vmem_limit_bytes=VMEM_LIMIT
        ),
        cost_estimate=pl.CostEstimate(flops=10**9, bytes_accessed=3 * 10**8, transcendentals=0),
        name="front",
    )(
        query_proj[0], key_proj[0], value_proj[0], init_state[0], out_gain[None, :], proj_weight,
        residual[0], moe_gain[None, :], expert_ids[0], gate_weights[0],
    )

    out = pl.pallas_call(
        expert_kernel,
        out_shape=jax.ShapeDtypeStruct((token_rows, D), BF16),
        in_specs=in_vmem(4),
        out_specs=pl.BlockSpec(memory_space=pltpu.VMEM),
        scratch_shapes=[
            pltpu.VMEM((slots, HALF), BF16),
            pltpu.VMEM((slots, HALF), BF16),
            pltpu.SemaphoreType.DMA,
            pltpu.SemaphoreType.DMA((count,)),
            pltpu.SemaphoreType.DMA((count,)),
        ],
        compiler_params=pltpu.CompilerParams(
            collective_id=2, has_side_effects=True, vmem_limit_bytes=VMEM_LIMIT
        ),
        cost_estimate=pl.CostEstimate(flops=5 * 10**9, bytes_accessed=2 * 10**8, transcendentals=0),
        name="experts",
    )(incoming, w_full, stream, weighing)
    return out[None]


def solution(mesh):
    placed = (
        P("expert", "seq", "head"),
        P("expert", "seq", "head"),
        P("expert", "seq", "head"),
        P("expert", "head", None, None),
        P("expert", ("seq", "head"), None),
        P("head"),
        P("head", "expert"),
        P(),
        P(("seq", "head"), None, "expert"),
        P(("seq", "head"), None, "expert"),
        P(("seq", "head"), None, "expert"),
        P("expert", ("seq", "head"), None),
        P("expert", ("seq", "head"), None),
    )
    nx, ny = grid_of(mesh.shape["seq"])
    return jax.shard_map(
        functools.partial(shards, nx, ny),
        mesh=mesh,
        in_specs=placed,
        out_specs=P("expert", ("seq", "head"), None),
        check_vma=False,
    )
```

time: 260 us -> 210 us (0.81)
  waiting for transfers between devices: 78 us -> 0.04 us
  Pallas kernels: 163 us -> 190 us
    all_gather x1, waiting for transfers between devices: 41.2 us -> 0.02 us  [shards(): w_full = lax.all_gather(stacked, 'expert', axis=1, tiled=True)]
    all_gather x1 -> x0, waiting for transfers between devices: 36 us -> none  [shards(): wo_full = lax.all_gather(proj_weight, 'expert', axis=1, tiled=True)]
    pallas_call x2 -> x1, Pallas kernels: 95.9 us -> 120 us  [shards(): pl.pallas_call(functools.partial(front_kernel, nx, ny, nz), out_shape=[ja...]
    pallas_call x1, Pallas kernels: 67.5 us -> 70.4 us  [shards(): pl.pallas_call(expert_kernel, out_shape=jax.ShapeDtypeStruct((token_rows,...]
  transfers between devices with their start and end apart: 2 -> 1, of which waited for: 2 -> 0; matrix products, arithmetic and copies ran while one was open for 1% -> 1% of each run, Pallas kernels for 37% -> 57%
where the time goes in v2:
time: 210 us; the launch traced here: 209 us
  Pallas kernels  190 us (90%)
  between operations  13.4 us (6%)
  local copies, waits for them, and re-layouts  3.08 us (1%)
  other arithmetic  2.28 us (1%)
    pallas_call x1, Pallas kernels, shards(): pl.pallas_call(functools.partial(front_kernel, nx, ny, nz), out_shape=[ja...  120 us
    pallas_call x1, Pallas kernels, shards(): pl.pallas_call(expert_kernel, out_shape=jax.ShapeDtypeStruct((token_rows,...  70.4 us
  transfers between devices with their start and end apart: 1, of which 0 were waited for; matrix products, arithmetic and copies ran while one was open for 1% of the time, Pallas kernels for 57%

profile of v2, /device:TPU:1, one launch (start us, length us, event | category | flops | bytes accessed | tf_op | source)
XLA Modules:
  0.0 209.3 jit_solution(11760601273961320546)
XLA Ops:
  6.5 0.0 copy-start
  6.5 0.0 copy-start.1
  6.5 0.0 all-gather.2.cloned.1.call-start
  6.5 2.3 %pad_maximum_fusion = bf16[2112,256]{1,0:T(8,128)(2,1)} fusion(bf16[704,256]{1,0:T(8,128)(2,1)} %bitcast.13, bf16[704,256]{1,0:T(8,128)(2,1)} %bitcast.14, bf16[704,256]{1,0:T(8,128)(2,1)} %bitcast.15), kind=kLoop, calls=%fused_computation | loop fusion | flops 3244032 | bytes 2162688 | tf_op jit(solution)/shard_map/concatenate | solution.py:428
  8.8 0.0 all-gather.2.cloned.1.call-update
  8.8 0.0 copy-done
  8.9 0.7 copy.14
  9.6 0.0 copy-done.1
  9.6 0.7 copy.15
  10.3 120.1 %front.1 = (bf16[64,2048]{1,0:T(8,128)(2,1)}, bf16[128,1024]{1,0:T(8,128)(2,1)}, bf16[1024,1024]{1,0:T(8,128)(2,1)}) custom-call(bf16[128,1024]{1,0:T(8,128)(2,1)} %bitcast.20, bf16[128,1024]{1,0:T(8,128)(2,1)} %bitcast.21, bf16[128,1024]{1,0:T(8,128)(2,1)} %bitcast.22, f32[8,128,128]{2,1,0:T(8,128)} %bitcast.19, f32[1,1024]{1,0:T(1,128)} %bitcast.25, ...), custom_call_target="tpu_custom_call" | custom-call | flops 1000000000 | bytes 300000000 | tf_op jit(solution)/shard_map/front/pallas_call | solution.py:435
  130.4 0.0 all-gather.2.cloned.1.call-done.w_ref
  130.4 70.4 %experts.1 = bf16[64,2048]{1,0:T(8,128)(2,1)} custom-call(bf16[1024,1024]{1,0:T(8,128)(2,1)} %get-tuple-element.8.x_ref, bf16[2112,2048]{1,0:T(8,128)(2,1)} %all-gather.2.cloned.1.call-done.w_ref, bf16[64,2048]{1,0:T(8,128)(2,1)} %get-tuple-element.9.stream_ref, bf16[128,1024]{1,0:T(8,128)(2,1)} %get-tuple-element.10.weigh_ref), custom_call_target="tpu_custom_call" | custom-call | flops 5000000000 | bytes 200000000 | tf_op jit(solution)/shard_map/experts/pallas_call | solution.py:475
  200.8 1.7 copy.17
Async XLA Ops:
  6.5 2.3 %copy-start = (s32[1,64,6]{1,0,2:T(1,128)S(1)}, s32[1,64,6]{1,0,2:T(1,128)}, u32[]{:S(2)}) copy-start(s32[1,64,6]{1,0,2:T(1,128)} %param.24) | copy-start | bytes 4612
  6.5 3.0 %copy-start.1 = (f32[1,64,6]{1,0,2:T(1,128)S(1)}, f32[1,64,6]{1,0,2:T(1,128)}, u32[]{:S(2)}) copy-start(f32[1,64,6]{1,0,2:T(1,128)} %param.25) | copy-start | bytes 4612
  6.5 123.9 %all-gather.2.cloned.1.call-start = ((), (), s32[]{:S(2)}) async-start(), calls=%async_computation | async-start | bytes 9732096 | tf_op jit(solution)/shard_map/all_gather | solution.py:429
Sparse Core Ops, SparseCore 0:
  9.4 110.9 all-gather.1

commit v3 on v2

--- a/solution.py
+++ b/solution.py
@@ -16,6 +16,7 @@
 MESH = pl.DeviceIdType.MESH
 BF16 = jnp.bfloat16
 F32 = jnp.float32
+CHUNKS = 2
 VMEM_LIMIT = 56 * 2**20
 
 
@@ -38,9 +39,16 @@
     )
 
 
-def place(ids_ref, gates_ref, placing, weighing):
+def position(dy, ny):
+    if dy == 0:
+        return ny - 1
+    return ny - 2 * dy if dy <= ny // 2 else 2 * dy - ny - 1
+
+
+def place(ids_ref, gates_ref, weighing):
     tokens = ids_ref.shape[0]
-    slots = placing.shape[1]
+    groups, _, group = weighing.shape
+    slots = groups * group
     experts = slots // BLK
     expert = lax.broadcasted_iota(jnp.int32, (tokens, experts), 1)
     chosen = jnp.zeros((tokens, experts), F32)
@@ -66,30 +74,32 @@
     for half in range(2):
         wanted = (place_in - (half * CAP - 1)).astype(F32)
         hit = (turn == wanted) & (place_in // CAP == half)
-        span = slice(half * tokens, (half + 1) * tokens)
-        placing[span, :] = jnp.where(hit, 1.0, 0.0).astype(BF16)
-        weighing[span, :] = jnp.where(hit, gates, 0.0).astype(BF16)
+        weights = jnp.where(hit, gates, 0.0).astype(BF16)
+        for i in range(groups):
+            weighing[i, half * tokens : (half + 1) * tokens, :] = weights[:, i * group : (i + 1) * group]
 
 
 def front_kernel(
     nx, ny, nz, q_ref, k_ref, v_ref, init_ref, out_gain_ref, wo_ref, res_ref, gain_ref, ids_ref, gates_ref,
     stream_ref, weigh_ref, incoming_ref,
-    loc, xin, tot, yin, pre, pin, att, mixed, wo, proj, snd, rcv, placing, feats, outgoing,
+    loc, xin, tot, yin, pre, pin, att, mixed, wo, proj, snd, rcv, own_weighing, weighing, feats, outgoing,
     x_send, x_recv, y_send, y_recv, p_send, p_recv, wz_send, wz_recv, wy_send, wy_recv,
-    right_send, right_recv, left_send, left_recv, pass_send, pass_recv, h_sem, own_sem, send, recv,
+    right_send, right_recv, left_send, left_recv, pass_send, pass_recv, h_sem, g_send, g_recv, own_sem,
+    f_send, f_recv, send, recv,
 ):
     s, h, z = lax.axis_index("seq"), lax.axis_index("head"), lax.axis_index("expert")
     y, x = s // nx, lax.rem(s, nx)
-    count = nx * ny * 2
-    me = s * 2 + h
+    across = 2 * nx
+    sub = x * 2 + h
     heads = q_ref.shape[1] // HD
     part = heads // nx
     tokens = res_ref.shape[0]
     depth = wo_ref.shape[0] // (nx * ny)
     width = wo_ref.shape[1]
 
-    def device(index):
-        return (index // 2, lax.rem(index, 2), z)
+    def at_sub(k):
+        other = lax.rem(sub + k, across)
+        return (y * nx + other // 2, lax.rem(other, 2), z)
 
     def at_x(d):
         return (y * nx + lax.rem(x + d, nx), h, z)
@@ -101,23 +111,17 @@
         return (s, h, lax.rem(z + d, nz))
 
     barrier = pltpu.get_barrier_semaphore()
-    for d in range(1, nz):
-        pl.semaphore_signal(barrier, inc=1, device_id=at_z(d), device_id_type=MESH)
-
-    def greet(off, carry):
-        pl.semaphore_signal(
-            barrier, inc=1, device_id=device(lax.rem(me + off, count)), device_id_type=MESH
-        )
-        return carry
-
-    with jax.named_scope("greet"):
-        lax.fori_loop(1, count, greet, 0)
+    peers = [at_z(d) for d in range(1, nz)]
+    peers += [at_y(d) for d in range(1, ny)]
+    peers += [at_sub(d) for d in range(1, across)]
+    for peer in peers:
+        pl.semaphore_signal(barrier, inc=1, device_id=peer, device_id_type=MESH)
     with jax.named_scope("states"):
         for i in range(heads):
             cols = slice(i * HD, (i + 1) * HD)
             loc[i // part, i % part] = dot(k_ref[:, cols], v_ref[:, cols], ((0,), (0,))).astype(BF16)
     with jax.named_scope("barrier"):
-        pl.semaphore_wait(barrier, count - 1 + nz - 1)
+        pl.semaphore_wait(barrier, len(peers))
 
     first = [
         remote(loc.at[lax.rem(x + d, nx)], xin.at[d], x_send.at[d], x_recv.at[d], at_x(d))
@@ -208,7 +212,16 @@
             scores = jnp.where(causal, scores, 0.0).astype(BF16)
             att[:, cols] = dot(scores, v_ref[:, cols])
     with jax.named_scope("placing"):
-        place(ids_ref, gates_ref, placing, weigh_ref)
+        place(ids_ref, gates_ref, own_weighing)
+        weighing[0] = own_weighing[y]
+        shared = [
+            remote(
+                own_weighing.at[lax.rem(y + d, ny)], weighing.at[d], g_send.at[d], g_recv.at[d], at_y(d)
+            )
+            for d in range(1, ny)
+        ]
+        for copy in shared:
+            copy.start()
     with jax.named_scope("relay_1"):
         relay_y(1)
         relay_y(ny - 1)
@@ -292,121 +305,231 @@
     stream_f = stream.astype(F32)
     inv = lax.rsqrt(jnp.mean(stream_f * stream_f, axis=1, keepdims=True) + 1e-06)
     moe_in = (stream_f * inv * gain_ref[...]).astype(BF16)
-    feats[:tokens, :] = moe_in[:, :HALF]
-    feats[tokens:, :] = moe_in[:, HALF:]
-    with jax.named_scope("outgoing"):
-        tile = 256
-        for c in range(outgoing.shape[0] // tile):
-            span = slice(c * tile, (c + 1) * tile)
-            outgoing[span, :] = dot(placing[:, span], feats[...], ((0,), (0,))).astype(BF16)
-
-    def block(off):
-        target = lax.rem(me + off, count)
+    chunks, wide = feats.shape[1], feats.shape[3]
+    for c in range(chunks):
+        feats[0, c, :tokens, :] = moe_in[:, c * wide : (c + 1) * wide]
+        feats[0, c, tokens:, :] = moe_in[:, HALF + c * wide : HALF + (c + 1) * wide]
+
+    def ring(b, c, step):
+        arrives = (b + step) % ny
+        sem = arrives * chunks + c
         return remote(
-            outgoing.at[rows(target, BLK), :], incoming_ref.at[rows(off, BLK), :],
-            send.at[off], recv.at[off], device(target),
-        )
-
-    def begin(off, carry):
-        block(off).start()
-        return carry
-
-    def finish(off, carry):
-        block(off).wait()
-        return carry
-
-    with jax.named_scope("begin"):
-        lax.fori_loop(1, count, begin, 0)
-    own = pltpu.make_async_copy(
-        outgoing.at[rows(me, BLK), :], incoming_ref.at[pl.ds(0, BLK), :], own_sem
-    )
-    own.start()
-    own.wait()
+            feats.at[b, c], feats.at[arrives, c], f_send.at[sem], f_recv.at[sem], at_y(step)
+        )
+
+    for c in range(chunks):
+        ring(0, c, 1).start()
+        ring(0, c, ny - 1).start()
+    for d in range(1, ny):
+        shared[d - 1].wait_recv()
+    weigh_ref[...] = weighing[...]
+
+    def block(b, k):
+        other = lax.rem(sub + k, across)
+        slot = position((ny - b) % ny, ny) * across + sub
+        sem = b * across + k
+        return remote(
+            outgoing.at[rows(b * across + other, BLK), :], incoming_ref.at[rows(slot, BLK), :],
+            send.at[sem], recv.at[sem], at_sub(k),
+        )
+
+    def arrived(b, k):
+        other = lax.rem(sub + across - k, across)
+        slot = position((ny - b) % ny, ny) * across + other
+        sem = b * across + k
+        return remote(
+            outgoing.at[rows(b * across + other, BLK), :], incoming_ref.at[rows(slot, BLK), :],
+            send.at[sem], recv.at[sem], at_sub(k),
+        )
+
+    def keep(b):
+        slot = position((ny - b) % ny, ny) * across + sub
+        return pltpu.make_async_copy(
+            outgoing.at[rows(b * across + sub, BLK), :], incoming_ref.at[rows(slot, BLK), :], own_sem.at[b]
+        )
+
+    group = across * BLK
+    around = [0]
+    for step in range(1, reach):
+        around += [step, ny - step]
+    around.append(reach)
+    for b in around:
+        picks = jnp.where(weighing[b].astype(F32) > 0.0, 1.0, 0.0).astype(BF16)
+        step = 1 if b <= reach else ny - 1
+        for c in range(chunks):
+            if b:
+                ring((b - step) % ny, c, step).wait_recv()
+                if b not in (reach, reach + 1):
+                    ring(b, c, step).start()
+            outgoing[b * group : (b + 1) * group, c * wide : (c + 1) * wide] = dot(
+                picks, feats[b, c], ((0,), (0,))
+            ).astype(BF16)
+
+        def begin(k, carry, b=b):
+            block(b, k).start()
+            return carry
+
+        lax.fori_loop(1, across, begin, 0)
+        keep(b).start()
+
     half.wait_send()
-    with jax.named_scope("arrivals"):
-        lax.fori_loop(1, count, finish, 0)
+    for copy in shared:
+        copy.wait_send()
+    for b in range(1, ny):
+        step = 1 if b <= reach else ny - 1
+        for c in range(chunks):
+            ring((b - step) % ny, c, step).wait_send()
+    for b in around:
+        keep(b).wait()
+
+        def finish(k, carry, b=b):
+            block(b, k).wait_send()
+            arrived(b, k).wait_recv()
+            return carry
+
+        lax.fori_loop(1, across, finish, 0)
 
 
 def expert_kernel(
-    x_ref, w_ref, stream_ref, weigh_ref, out_ref, results, returned, own_sem, send, recv
+    nx, ny, x_ref, w_ref, stream_ref, weigh_ref, out_ref, results, returned, right_out, right_in, left_out, left_in,
+    send, recv, right_send, right_recv, left_send, left_recv,
 ):
     s, h, z = lax.axis_index("seq"), lax.axis_index("head"), lax.axis_index("expert")
-    count = lax.axis_size("seq") * lax.axis_size("head")
-    me = s * 2 + h
+    y, x = s // nx, lax.rem(s, nx)
+    across = 2 * nx
+    sub = x * 2 + h
+    reach = ny // 2
+    group = across * BLK
     tokens = stream_ref.shape[0]
     hidden_width = w_ref.shape[0] // 3
-
-    def device(index):
-        return (index // 2, lax.rem(index, 2), z)
+    chunks, wide = right_out.shape[1], right_out.shape[3]
+
+    def at_sub(k):
+        other = lax.rem(sub + k, across)
+        return (y * nx + other // 2, lax.rem(other, 2), z)
+
+    def at_y(d):
+        return (lax.rem(y + d, ny) * nx + x, h, z)
 
     barrier = pltpu.get_barrier_semaphore()
-
-    def greet(off, carry):
-        pl.semaphore_signal(
-            barrier, inc=1, device_id=device(lax.rem(me + off, count)), device_id_type=MESH
-        )
-        return carry
-
-    with jax.named_scope("greet"):
-        lax.fori_loop(1, count, greet, 0)
-
-    def block(off):
+    peers = [at_y(1), at_y(ny - 1), *[at_sub(k) for k in range(1, across)]]
+    for peer in peers:
+        pl.semaphore_signal(barrier, inc=1, device_id=peer, device_id_type=MESH)
+
+    def block(p, k, source):
+        slot = p * across + lax.rem(sub + k, across)
+        sem = p * across + k
         return remote(
-            results.at[rows(off, BLK), :], returned.at[rows(me, BLK), :],
-            send.at[off], recv.at[off], device(lax.rem(me + count - off, count)),
-        )
-
-    def begin(off, carry):
-        block(off).start()
-        return carry
-
-    with jax.named_scope("experts"):
-        group = count // 2
-        for c in range(2):
-            span = slice(c * group * BLK, (c + 1) * group * BLK)
-            x = x_ref[span, :].astype(F32).reshape(group, BLK, HALF)
-            low = x[:, :CAP].reshape(group * CAP, HALF).astype(BF16)
-            high = x[:, CAP:].reshape(group * CAP, HALF).astype(BF16)
-            acts = []
-            for i in range(2):
-                span_w = slice(i * hidden_width, (i + 1) * hidden_width)
-                acts.append(
-                    dot(low, w_ref[span_w, :HALF], ((1,), (1,)))
-                    + dot(high, w_ref[span_w, HALF:], ((1,), (1,)))
-                )
-            gate, up = acts
-            hidden = (gate / (1.0 + jnp.exp(-gate)) * up).astype(BF16)
-            outs = [
-                dot(hidden, w_ref[2 * hidden_width :, i * HALF : (i + 1) * HALF]).reshape(group, CAP, HALF)
-                for i in range(2)
-            ]
-            results[span, :] = jnp.concatenate(outs, axis=1).reshape(group * BLK, HALF).astype(BF16)
-            if c == 0:
-                pl.semaphore_wait(barrier, count - 1)
-            lax.fori_loop(max(1, c * group), (c + 1) * group, begin, 0)
-    own = pltpu.make_async_copy(
-        results.at[pl.ds(0, BLK), :], returned.at[rows(me, BLK), :], own_sem
-    )
-    own.start()
-    own.wait()
-
-    def finish(off, carry):
-        source = lax.rem(me + off, count)
-        block(off).wait_send()
-        remote(
-            results.at[rows(off, BLK), :], returned.at[rows(source, BLK), :],
-            send.at[off], recv.at[off], device(source),
-        ).wait_recv()
-        return carry
-
-    with jax.named_scope("arrivals"):
-        lax.fori_loop(1, count, finish, 0)
-    with jax.named_scope("combine"):
-        combined = dot(weigh_ref[...], returned[...])
+            results.at[rows(slot, BLK), :], returned.at[rows(p * across + source, BLK), :],
+            send.at[sem], recv.at[sem], at_sub(k),
+        )
+
+    def compute(g):
+        span = slice(2 * g * group, 2 * (g + 1) * group)
+        blocks = x_ref[span, :].astype(F32).reshape(2 * across, BLK, HALF)
+        low = blocks[:, :CAP].reshape(2 * across * CAP, HALF).astype(BF16)
+        high = blocks[:, CAP:].reshape(2 * across * CAP, HALF).astype(BF16)
+        acts = []
+        for i in range(2):
+            part = slice(i * hidden_width, (i + 1) * hidden_width)
+            acts.append(
+                dot(low, w_ref[part, :HALF], ((1,), (1,)))
+                + dot(high, w_ref[part, HALF:], ((1,), (1,)))
+            )
+        gate, up = acts
+        hidden = (gate / (1.0 + jnp.exp(-gate)) * up).astype(BF16)
+        outs = [
+            dot(hidden, w_ref[2 * hidden_width :, i * HALF : (i + 1) * HALF]).reshape(
+                2 * across, CAP, HALF
+            )
+            for i in range(2)
+        ]
+        results[span, :] = (
+            jnp.concatenate(outs, axis=1).reshape(2 * across * BLK, HALF).astype(BF16)
+        )
+        if g == 0:
+            pl.semaphore_wait(barrier, len(peers))
+        for p in (2 * g, 2 * g + 1):
+
+            def begin(k, carry, p=p):
+                block(p, k, sub).start()
+                return carry
+
+            lax.fori_loop(1, across, begin, 0)
+            own = rows(p * across + sub, BLK)
+            returned[own, :] = results[own, :]
+
+    def landed(p):
+        def one(k, carry):
+            block(p, k, lax.rem(sub + across - k, across)).wait_recv()
+            return carry
+
+        lax.fori_loop(1, across, one, 0)
+
+    def weighed(dy, c):
+        p = position(dy, ny)
+        return dot(
+            weigh_ref[(ny - dy) % ny],
+            returned[p * group : (p + 1) * group, c * wide : (c + 1) * wide],
+        )
+
+    def to_right(step, c):
+        sem = step * chunks + c
+        return remote(
+            right_out.at[step, c], right_in.at[step, c], right_send.at[sem], right_recv.at[sem], at_y(1)
+        )
+
+    def to_left(step, c):
+        sem = step * chunks + c
+        return remote(
+            left_out.at[step, c], left_in.at[step, c], left_send.at[sem], left_recv.at[sem], at_y(ny - 1)
+        )
+
+    def advance(step):
+        for dy, to, outbox, inbox in (
+            (reach - step, to_right, right_out, right_in),
+            (reach + 1 + step, to_left, left_out, left_in),
+        ):
+            if dy == ny:
+                continue
+            landed(position(dy, ny))
+            for c in range(chunks):
+                total = weighed(dy, c)
+                if step:
+                    to(step - 1, c).wait_recv()
+                    total = total + inbox[step - 1, c].astype(F32)
+                outbox[step, c] = total.astype(BF16)
+                to(step, c).start()
+
+    for g in range(ny // 2):
+        compute(g)
+        if g:
+            advance(g - 1)
+    for step in range(ny // 2 - 1, reach):
+        advance(step)
+    landed(ny - 1)
+    for c in range(chunks):
+        total = weighed(0, c)
+        to_right(reach - 1, c).wait_recv()
+        to_left(reach - 2, c).wait_recv()
+        total = total + right_in[reach - 1, c].astype(F32) + left_in[reach - 2, c].astype(F32)
         for half in range(2):
-            cols = slice(half * HALF, (half + 1) * HALF)
-            span = slice(half * tokens, (half + 1) * tokens)
-            out_ref[:, cols] = (stream_ref[:, cols].astype(F32) + combined[span, :]).astype(BF16)
+            cols = slice(half * HALF + c * wide, half * HALF + (c + 1) * wide)
+            out_ref[:, cols] = (
+                stream_ref[:, cols].astype(F32) + total[half * tokens : (half + 1) * tokens, :]
+            ).astype(BF16)
+    for c in range(chunks):
+        for step in range(reach):
+            to_right(step, c).wait_send()
+        for step in range(reach - 1):
+            to_left(step, c).wait_send()
+    for p in range(ny):
+
+        def finish(k, carry, p=p):
+            block(p, k, sub).wait_send()
+            return carry
+
+        lax.fori_loop(1, across, finish, 0)
 
 
 def in_vmem(n):
@@ -424,6 +547,7 @@
     token_rows = residual.shape[1]
     count = nx * ny * 2
     slots = count * BLK
+    group = 2 * nx * BLK
 
     stacked = jnp.concatenate([w_gate[0], w_up[0], w_down[0]], axis=0)
     w_full = lax.all_gather(stacked, "expert", axis=1, tiled=True)
@@ -436,7 +560,7 @@
         functools.partial(front_kernel, nx, ny, nz),
         out_shape=[
             jax.ShapeDtypeStruct((token_rows, D), BF16),
-            jax.ShapeDtypeStruct((2 * token_rows, slots), BF16),
+            jax.ShapeDtypeStruct((ny, 2 * token_rows, group), BF16),
             jax.ShapeDtypeStruct((slots, HALF), BF16),
         ],
         in_specs=in_vmem(10),
@@ -454,13 +578,12 @@
             pltpu.VMEM((tok, D), F32),
             pltpu.VMEM((token_rows, D), BF16),
             pltpu.VMEM((token_rows, D), BF16),
-            pltpu.VMEM((2 * token_rows, slots), BF16),
-            pltpu.VMEM((2 * token_rows, HALF), BF16),
+            pltpu.VMEM((ny, 2 * token_rows, group), BF16),
+            pltpu.VMEM((ny, 2 * token_rows, group), BF16),
+            pltpu.VMEM((ny, CHUNKS, 2 * token_rows, HALF // CHUNKS), BF16),
             pltpu.VMEM((slots, HALF), BF16),
             *[dma((n,)) for n in (nx, nx, ny, ny, nx, nx, nz, nz, ny, ny, ny, ny, ny, ny, ny, ny, 2)],
-            dma,
-            dma((count,)),
-            dma((count,)),
+            *[dma((n,)) for n in (ny, ny, ny, ny * CHUNKS, ny * CHUNKS, count, count)],
         ],
         compiler_params=pltpu.CompilerParams(
             collective_id=0, has_side_effects=True, vmem_limit_bytes=VMEM_LIMIT
@@ -472,17 +595,18 @@
         residual[0], moe_gain[None, :], expert_ids[0], gate_weights[0],
     )
 
+    passing = (CHUNKS, 2 * token_rows, HALF // CHUNKS)
     out = pl.pallas_call(
-        expert_kernel,
+        functools.partial(expert_kernel, nx, ny),
         out_shape=jax.ShapeDtypeStruct((token_rows, D), BF16),
         in_specs=in_vmem(4),
         out_specs=pl.BlockSpec(memory_space=pltpu.VMEM),
         scratch_shapes=[
             pltpu.VMEM((slots, HALF), BF16),
             pltpu.VMEM((slots, HALF), BF16),
-            pltpu.SemaphoreType.DMA,
-            pltpu.SemaphoreType.DMA((count,)),
-            pltpu.SemaphoreType.DMA((count,)),
+            *[pltpu.VMEM((n, *passing), BF16) for n in (ny // 2, ny // 2, ny // 2 - 1, ny // 2 - 1)],
+            *[dma((n,)) for n in (count, count)],
+            *[dma((n * CHUNKS,)) for n in (ny // 2, ny // 2, ny // 2 - 1, ny // 2 - 1)],
         ],
         compiler_params=pltpu.CompilerParams(
             collective_id=2, has_side_effects=True, vmem_limit_bytes=VMEM_LIMIT

time: 210 us -> 175 us (0.83)
  Pallas kernels: 190 us -> 155 us
    pallas_call x1, Pallas kernels: 70.4 us -> 47.9 us  [shards(): pl.pallas_call(functools.partial(expert_kernel, nx, ny), out_shape=jax.Sh...]
    pallas_call x1, Pallas kernels: 120 us -> 107 us  [shards(): pl.pallas_call(functools.partial(front_kernel, nx, ny, nz), out_shape=[ja...]
  transfers between devices with their start and end apart: 1 -> 1, of which waited for: 0 -> 1; matrix products, arithmetic and copies ran while one was open for 1% -> 1% of each run, Pallas kernels for 57% -> 61%
where the time goes in v3:
time: 175 us
  Pallas kernels  155 us (89%)
  between operations  13.4 us (8%)
  local copies, waits for them, and re-layouts  3.08 us (2%)
  other arithmetic  2.28 us (1%)
    pallas_call x1, Pallas kernels, shards(): pl.pallas_call(functools.partial(front_kernel, nx, ny, nz), out_shape=[ja...  107 us
    pallas_call x1, Pallas kernels, shards(): pl.pallas_call(functools.partial(expert_kernel, nx, ny), out_shape=jax.Sh...  47.9 us
  transfers between devices with their start and end apart: 1, of which 1 were waited for; matrix products, arithmetic and copies ran while one was open for 1% of the time, Pallas kernels for 61%

profile of v3, /device:TPU:1, one launch (start us, length us, event | category | flops | bytes accessed | tf_op | source)
XLA Modules:
  0.0 175.2 jit_solution(8729602115441665204)
XLA Ops:
  6.5 0.0 copy-start
  6.5 0.0 copy-start.1
  6.5 0.0 all-gather.2.cloned.1.call-start
  6.5 2.3 %pad_maximum_fusion = bf16[2112,256]{1,0:T(8,128)(2,1)} fusion(bf16[704,256]{1,0:T(8,128)(2,1)} %bitcast.13, bf16[704,256]{1,0:T(8,128)(2,1)} %bitcast.14, bf16[704,256]{1,0:T(8,128)(2,1)} %bitcast.15), kind=kLoop, calls=%fused_computation | loop fusion | flops 3244032 | bytes 2162688 | tf_op jit(solution)/shard_map/concatenate | solution.py:552
  8.8 0.0 all-gather.2.cloned.1.call-update
  8.8 0.0 copy-done
  8.9 0.7 copy.14
  9.6 0.0 copy-done.1
  9.6 0.7 copy.15
  10.3 107.1 %front.1 = (bf16[64,2048]{1,0:T(8,128)(2,1)}, bf16[8,128,128]{2,1,0:T(8,128)(2,1)}, bf16[1024,1024]{1,0:T(8,128)(2,1)}) custom-call(bf16[128,1024]{1,0:T(8,128)(2,1)} %bitcast.20, bf16[128,1024]{1,0:T(8,128)(2,1)} %bitcast.21, bf16[128,1024]{1,0:T(8,128)(2,1)} %bitcast.22, f32[8,128,128]{2,1,0:T(8,128)} %bitcast.19, f32[1,1024]{1,0:T(1,128)} %bitcast.25, ...), custom_call_target="tpu_custom_call" | custom-call | flops 1000000000 | bytes 300000000 | tf_op jit(solution)/shard_map/front/pallas_call | solution.py:559
  117.3 1.4 all-gather.2.cloned.1.call-done.w_ref
  118.7 47.9 %experts.1 = bf16[64,2048]{1,0:T(8,128)(2,1)} custom-call(bf16[1024,1024]{1,0:T(8,128)(2,1)} %get-tuple-element.8.x_ref, bf16[2112,2048]{1,0:T(8,128)(2,1)} %all-gather.2.cloned.1.call-done.w_ref, bf16[64,2048]{1,0:T(8,128)(2,1)} %get-tuple-element.9.stream_ref, bf16[8,128,128]{2,1,0:T(8,128)(2,1)} %get-tuple-element.10.weigh_ref), custom_call_target="tpu_custom_call" | custom-call | flops 5000000000 | bytes 200000000 | tf_op jit(solution)/shard_map/experts/pallas_call | solution.py:599
  166.7 1.7 copy.17
Async XLA Ops:
  6.5 2.3 %copy-start = (s32[1,64,6]{1,0,2:T(1,128)S(1)}, s32[1,64,6]{1,0,2:T(1,128)}, u32[]{:S(2)}) copy-start(s32[1,64,6]{1,0,2:T(1,128)} %param.24) | copy-start | bytes 4612
  6.5 3.0 %copy-start.1 = (f32[1,64,6]{1,0,2:T(1,128)S(1)}, f32[1,64,6]{1,0,2:T(1,128)}, u32[]{:S(2)}) copy-start(f32[1,64,6]{1,0,2:T(1,128)} %param.25) | copy-start | bytes 4612
  6.5 112.2 %all-gather.2.cloned.1.call-start = ((), (), s32[]{:S(2)}) async-start(), calls=%async_computation | async-start | bytes 9732096 | tf_op jit(solution)/shard_map/all_gather | solution.py:553
Sparse Core Ops, SparseCore 0:
  9.4 109.3 all-gather.1

commit v4 on v3

--- a/solution.py
+++ b/solution.py
@@ -45,30 +45,40 @@
     return ny - 2 * dy if dy <= ny // 2 else 2 * dy - ny - 1
 
 
+def way(b, c, n):
+    return 1 if b < n // 2 or (b == n // 2 and c == 0) else n - 1
+
+
+def onward(b, c, n):
+    step = way(b, c, n)
+    further = (b + step) % n
+    return step if further and way(further, c, n) == step else None
+
+
 def place(ids_ref, gates_ref, weighing):
-    tokens = ids_ref.shape[0]
+    tokens = ids_ref.shape[2]
     groups, _, group = weighing.shape
     slots = groups * group
     experts = slots // BLK
-    expert = lax.broadcasted_iota(jnp.int32, (tokens, experts), 1)
-    chosen = jnp.zeros((tokens, experts), F32)
-    gates = jnp.zeros((tokens, experts), F32)
+    expert = lax.broadcasted_iota(jnp.int32, (experts, tokens), 0)
+    chosen = jnp.zeros((experts, tokens), F32)
+    gates = jnp.zeros((experts, tokens), F32)
     for k in range(TOP):
-        match = ids_ref[:, k : k + 1] == expert
+        match = ids_ref[k] == expert
         chosen = chosen + jnp.where(match, 1.0, 0.0)
-        gates = gates + jnp.where(match, gates_ref[:, k : k + 1], 0.0)
-    earlier = lax.broadcasted_iota(jnp.int32, (tokens, tokens), 1) < lax.broadcasted_iota(
-        jnp.int32, (tokens, tokens), 0
+        gates = gates + jnp.where(match, gates_ref[k], 0.0)
+    earlier = lax.broadcasted_iota(jnp.int32, (tokens, tokens), 0) < lax.broadcasted_iota(
+        jnp.int32, (tokens, tokens), 1
     )
     earlier = jnp.where(earlier, 1.0, 0.0).astype(BF16)
-    order = dot(earlier, chosen.astype(BF16))
+    order = dot(chosen.astype(BF16), earlier)
     turn = (chosen * (order + 1.0)).astype(BF16)
     spread = lax.broadcasted_iota(jnp.int32, (experts, slots), 1) // BLK == lax.broadcasted_iota(
         jnp.int32, (experts, slots), 0
     )
     spread = jnp.where(spread, 1.0, 0.0).astype(BF16)
-    turn = dot(turn, spread)
-    gates = dot(gates.astype(BF16), spread)
+    turn = dot(turn, spread, ((0,), (0,)))
+    gates = dot(gates.astype(BF16), spread, ((0,), (0,)))
     slot = lax.broadcasted_iota(jnp.int32, (tokens, slots), 1)
     place_in = lax.rem(slot, BLK)
     for half in range(2):
@@ -80,12 +90,12 @@
 
 
 def front_kernel(
-    nx, ny, nz, q_ref, k_ref, v_ref, init_ref, out_gain_ref, wo_ref, res_ref, gain_ref, ids_ref, gates_ref,
-    stream_ref, weigh_ref, incoming_ref,
+    nx, ny, nz, q_ref, k_ref, v_ref, init_ref, out_gain_ref, wo_ref, res_ref, gain_ref, ids_ref, gates_ref, gate_ref, up_ref, down_ref,
+    stream_ref, weigh_ref, incoming_ref, gate_full_ref, up_full_ref, down_full_ref,
     loc, xin, tot, yin, pre, pin, att, mixed, wo, proj, snd, rcv, own_weighing, weighing, feats, outgoing,
     x_send, x_recv, y_send, y_recv, p_send, p_recv, wz_send, wz_recv, wy_send, wy_recv,
     right_send, right_recv, left_send, left_recv, pass_send, pass_recv, h_sem, g_send, g_recv, own_sem,
-    f_send, f_recv, send, recv,
+    f_send, f_recv, send, recv, bx_send, bx_recv, by_send, by_recv, ring_send, ring_recv, ring_own,
 ):
     s, h, z = lax.axis_index("seq"), lax.axis_index("head"), lax.axis_index("expert")
     y, x = s // nx, lax.rem(s, nx)
@@ -94,8 +104,9 @@
     heads = q_ref.shape[1] // HD
     part = heads // nx
     tokens = res_ref.shape[0]
-    depth = wo_ref.shape[0] // (nx * ny)
-    width = wo_ref.shape[1]
+    depth, width = wo.shape[3:]
+    reach = ny // 2
+    cross = 6 * nz // 8
 
     def at_sub(k):
         other = lax.rem(sub + k, across)
@@ -130,35 +141,92 @@
     for copy in first:
         copy.start()
 
-    def strip(dx, dy):
-        return pl.ds(
-            pl.multiple_of((lax.rem(x + dx, nx) * ny + lax.rem(y + dy, ny)) * depth, depth), depth
-        )
-
-    mine = strip(0, 0)
+    shares = (gate_ref, up_ref, down_ref)
+    fulls = (gate_full_ref, up_full_ref, down_full_ref)
+    pieces = 2 * len(shares)
+    half_rows = gate_ref.shape[0] // 2
+
+    def piece(b, i, step):
+        span = pl.ds(i % 2 * half_rows, half_rows)
+        there = fulls[i // 2].at[lax.rem(z + nz - b, nz), span, :]
+        sem = (b + step) % nz * pieces + i
+        return remote(
+            there if b else shares[i // 2].at[span, :], there, ring_send.at[sem], ring_recv.at[sem], at_z(step)
+        )
+
+    def piece_came(b, i):
+        span = pl.ds(i % 2 * half_rows, half_rows)
+        there = fulls[i // 2].at[lax.rem(z + nz - b, nz), span, :]
+        sem = b * pieces + i
+        return remote(there, there, ring_send.at[sem], ring_recv.at[sem], at_z(1))
+
+    def relay_ring(distance, later):
+        for i in range(later * pieces // 2, (later + 1) * pieces // 2):
+            for b in sorted({distance, nz - distance}):
+                piece_came(b, i).wait_recv()
+                step = onward(b, later, nz)
+                if step:
+                    piece(b, i, step).start()
+
+    mine = rows(x * ny + y, depth)
 
     def fetch(d, owner):
         return remote(
-            wo_ref.at[mine, :], wo.at[owner, mine, :], wz_send.at[d], wz_recv.at[d], at_z(d)
+            wo_ref.at[mine, :], wo.at[owner, x, y], wz_send.at[d], wz_recv.at[d], at_z(d)
         )
 
     for d in range(1, nz):
         fetch(d, z).start()
+    for i in range(pieces):
+        for step in (1, nz - 1):
+            piece(0, i, step).start()
+    kept = [
+        pltpu.make_async_copy(share, full.at[z], ring_own.at[i])
+        for i, (share, full) in enumerate(zip(shares, fulls, strict=True))
+    ]
+    for copy in kept:
+        copy.start()
+
+    def chip(dx, b):
+        return wo.at[pl.ds(0, cross), lax.rem(x + dx, nx), lax.rem(y + ny - b, ny)]
 
     def along_y(b, step):
-        block = wo.at[:, strip(0, ny - b), :]
         arrives = (b + step) % ny
-        return remote(block, block, wy_send.at[arrives], wy_recv.at[arrives], at_y(step))
-
-    def landed_y(b, step):
-        block = wo.at[:, strip(0, ny - b), :]
-        return remote(block, block, wy_send.at[b], wy_recv.at[b], at_y(step))
+        return remote(chip(0, b), chip(0, b), wy_send.at[arrives], wy_recv.at[arrives], at_y(step))
+
+    def landed_y(b):
+        return remote(chip(0, b), chip(0, b), wy_send.at[b], wy_recv.at[b], at_y(1))
 
     def along_x(b, dx, sends, recvs, step):
-        block = wo.at[:, strip(dx, ny - b), :]
-        return remote(block, block, sends.at[b], recvs.at[b], at_x(step))
-
-    reach = ny // 2
+        return remote(chip(dx, b), chip(dx, b), sends.at[b], recvs.at[b], at_x(step))
+
+    rest = pl.ds(cross, nz - cross)
+
+    def side(d):
+        own = wo.at[rest, x, y]
+        return remote(own, own, bx_send.at[d], bx_recv.at[d], at_x(d))
+
+    def side_came(d):
+        there = wo.at[rest, lax.rem(x + nx - d, nx), y]
+        return remote(there, there, bx_send.at[d], bx_recv.at[d], at_x(d))
+
+    def row(b, c, step):
+        part_of = wo.at[rest, pl.ds(c * (nx // 2), nx // 2), lax.rem(y + ny - b, ny)]
+        sem = (b + step) % ny * 2 + c
+        return remote(part_of, part_of, by_send.at[sem], by_recv.at[sem], at_y(step))
+
+    def row_came(b, c):
+        there = wo.at[rest, pl.ds(c * (nx // 2), nx // 2), lax.rem(y + ny - b, ny)]
+        sem = b * 2 + c
+        return remote(there, there, by_send.at[sem], by_recv.at[sem], at_y(1))
+
+    def relay_row(b):
+        for c in range(2):
+            row_came(b, c).wait_recv()
+            step = onward(b, c, ny)
+            if step:
+                row(b, c, step).start()
+
     to_right = [0, *range(reach + 1, ny)]
 
     def spread(b):
@@ -166,14 +234,11 @@
         along_x(b, 0, left_send, left_recv, nx - 1).start()
 
     def relay_y(b):
-        if b <= reach:
-            landed_y(b, 1).wait_recv()
-            if b < reach:
-                along_y(b, 1).start()
-        else:
-            landed_y(b, ny - 1).wait_recv()
-            if b > reach + 1:
-                along_y(b, ny - 1).start()
+        landed_y(b).wait_recv()
+        if b < reach:
+            along_y(b, 1).start()
+        elif b > reach + 1:
+            along_y(b, ny - 1).start()
         spread(b)
 
     def relay_x(b):
@@ -194,11 +259,13 @@
         copy.start()
 
     with jax.named_scope("fetched"):
-        wo[z, mine, :] = wo_ref[mine, :]
+        wo[z, x, y] = wo_ref[mine, :]
         for d in range(1, nz):
             fetch(d, lax.rem(z + nz - d, nz)).wait_recv()
     along_y(0, 1).start()
     along_y(0, ny - 1).start()
+    for d in range(1, nx):
+        side(d).start()
     spread(0)
 
     with jax.named_scope("inner"):
@@ -213,19 +280,18 @@
             att[:, cols] = dot(scores, v_ref[:, cols])
     with jax.named_scope("placing"):
         place(ids_ref, gates_ref, own_weighing)
-        weighing[0] = own_weighing[y]
-        shared = [
-            remote(
-                own_weighing.at[lax.rem(y + d, ny)], weighing.at[d], g_send.at[d], g_recv.at[d], at_y(d)
-            )
-            for d in range(1, ny)
-        ]
-        for copy in shared:
-            copy.start()
     with jax.named_scope("relay_1"):
+        for d in range(1, nx):
+            side_came(d).wait_recv()
+        for c in range(2):
+            for step in (1, ny - 1):
+                row(0, c, step).start()
         relay_y(1)
         relay_y(ny - 1)
         relay_x(0)
+        relay_row(1)
+        relay_row(ny - 1)
+        relay_ring(1, 0)
 
     before = jnp.zeros(tot.shape, F32)
     with jax.named_scope("states_y"):
@@ -249,11 +315,24 @@
         for step in range(2, reach):
             relay_y(step)
             relay_y(ny - step)
+            relay_row(step)
+            relay_row(ny - step)
             relay_x(step - 1)
             relay_x(ny - step + 1)
         relay_y(reach)
+        relay_row(reach)
         relay_x(reach - 1)
         relay_x(reach + 1)
+        relay_ring(1, 1)
+    weighing[0] = own_weighing[y]
+    shared = [
+        remote(
+            own_weighing.at[lax.rem(y + d, ny)], weighing.at[d], g_send.at[d], g_recv.at[d], at_y(d)
+        )
+        for d in range(1, ny)
+    ]
+    for copy in shared:
+        copy.start()
     with jax.named_scope("mix"):
         for e in range(nx):
             if e:
@@ -275,12 +354,14 @@
                 along_x(b, nx - 1, right_send, right_recv, 1).wait_recv()
                 along_x(b, 2, pass_send, pass_recv, nx - 1).wait_recv()
 
+    relay_ring(2, 0)
     with jax.named_scope("project"):
         for c in range(nz):
-            proj[:, c * width : (c + 1) * width] = dot(mixed[...], wo[c])
+            proj[:, c * width : (c + 1) * width] = dot(mixed[...], wo[c].reshape(nx * ny * depth, width))
     snd[...] = proj[rows(1 - h, tokens), :].astype(BF16)
     half = remote(snd, rcv, h_sem.at[0], h_sem.at[1], (s, 1 - h, z))
     half.start()
+    relay_ring(2, 1)
     for copy in first + second + third:
         copy.wait_send()
     for d in range(1, nz):
@@ -296,6 +377,11 @@
             along_y(b - 1, 1).wait_send()
         elif b:
             along_y((b + 1) % ny, ny - 1).wait_send()
+        if b:
+            for c in range(2):
+                row_came(b, c).wait_send()
+    for d in range(1, nx):
+        side(d).wait_send()
     with jax.named_scope("other_half"):
         half.wait_recv()
     stream = (
@@ -354,12 +440,17 @@
         around += [step, ny - step]
     around.append(reach)
     for b in around:
+        if b == 2:
+            relay_ring(3, 0)
+        if b == reach:
+            relay_ring(3, 1)
         picks = jnp.where(weighing[b].astype(F32) > 0.0, 1.0, 0.0).astype(BF16)
-        step = 1 if b <= reach else ny - 1
         for c in range(chunks):
             if b:
+                step = way(b, c, ny)
                 ring((b - step) % ny, c, step).wait_recv()
-                if b not in (reach, reach + 1):
+                step = onward(b, c, ny)
+                if step:
                     ring(b, c, step).start()
             outgoing[b * group : (b + 1) * group, c * wide : (c + 1) * wide] = dot(
                 picks, feats[b, c], ((0,), (0,))
@@ -376,9 +467,16 @@
     for copy in shared:
         copy.wait_send()
     for b in range(1, ny):
-        step = 1 if b <= reach else ny - 1
         for c in range(chunks):
+            step = way(b, c, ny)
             ring((b - step) % ny, c, step).wait_send()
+    for later in range(2):
+        relay_ring(nz // 2, later)
+    for copy in kept:
+        copy.wait()
+    for b in range(1, nz):
+        for i in range(pieces):
+            piece_came(b, i).wait_send()
     for b in around:
         keep(b).wait()
 
@@ -391,7 +489,7 @@
 
 
 def expert_kernel(
-    nx, ny, x_ref, w_ref, stream_ref, weigh_ref, out_ref, results, returned, right_out, right_in, left_out, left_in,
+    nx, ny, x_ref, gate_ref, up_ref, down_ref, stream_ref, weigh_ref, out_ref, results, returned, right_out, right_in, left_out, left_in,
     send, recv, right_send, right_recv, left_send, left_recv,
 ):
     s, h, z = lax.axis_index("seq"), lax.axis_index("head"), lax.axis_index("expert")
@@ -401,7 +499,8 @@
     reach = ny // 2
     group = across * BLK
     tokens = stream_ref.shape[0]
-    hidden_width = w_ref.shape[0] // 3
+    many = ny // 2
+    shards_in_half = down_ref.shape[0] // 2
     chunks, wide = right_out.shape[1], right_out.shape[3]
 
     def at_sub(k):
@@ -425,31 +524,35 @@
         )
 
     def compute(g):
-        span = slice(2 * g * group, 2 * (g + 1) * group)
-        blocks = x_ref[span, :].astype(F32).reshape(2 * across, BLK, HALF)
-        low = blocks[:, :CAP].reshape(2 * across * CAP, HALF).astype(BF16)
-        high = blocks[:, CAP:].reshape(2 * across * CAP, HALF).astype(BF16)
+        span = slice(many * g * group, many * (g + 1) * group)
+        blocks = x_ref[span, :].astype(F32).reshape(many * across, BLK, HALF)
+        low = blocks[:, :CAP].reshape(many * across * CAP, HALF).astype(BF16)
+        high = blocks[:, CAP:].reshape(many * across * CAP, HALF).astype(BF16)
         acts = []
-        for i in range(2):
-            part = slice(i * hidden_width, (i + 1) * hidden_width)
-            acts.append(
-                dot(low, w_ref[part, :HALF], ((1,), (1,)))
-                + dot(high, w_ref[part, HALF:], ((1,), (1,)))
-            )
+        for w_ref in (gate_ref, up_ref):
+            total = None
+            for i, values in enumerate((low, high)):
+                for j in range(shards_in_half):
+                    wide_in = HALF // shards_in_half
+                    term = dot(
+                        values[:, j * wide_in : (j + 1) * wide_in], w_ref[i * shards_in_half + j], ((1,), (1,))
+                    )
+                    total = term if total is None else total + term
+            acts.append(total)
         gate, up = acts
         hidden = (gate / (1.0 + jnp.exp(-gate)) * up).astype(BF16)
         outs = [
-            dot(hidden, w_ref[2 * hidden_width :, i * HALF : (i + 1) * HALF]).reshape(
-                2 * across, CAP, HALF
-            )
+            jnp.concatenate(
+                [dot(hidden, down_ref[i * shards_in_half + j]) for j in range(shards_in_half)], axis=1
+            ).reshape(many * across, CAP, HALF)
             for i in range(2)
         ]
         results[span, :] = (
-            jnp.concatenate(outs, axis=1).reshape(2 * across * BLK, HALF).astype(BF16)
+            jnp.concatenate(outs, axis=1).reshape(many * across * BLK, HALF).astype(BF16)
         )
         if g == 0:
             pl.semaphore_wait(barrier, len(peers))
-        for p in (2 * g, 2 * g + 1):
+        for p in range(many * g, many * (g + 1)):
 
             def begin(k, carry, p=p):
                 block(p, k, sub).start()
@@ -485,44 +588,43 @@
             left_out.at[step, c], left_in.at[step, c], left_send.at[sem], left_recv.at[sem], at_y(ny - 1)
         )
 
-    def advance(step):
-        for dy, to, outbox, inbox in (
-            (reach - step, to_right, right_out, right_in),
-            (reach + 1 + step, to_left, left_out, left_in),
-        ):
-            if dy == ny:
-                continue
-            landed(position(dy, ny))
-            for c in range(chunks):
-                total = weighed(dy, c)
-                if step:
-                    to(step - 1, c).wait_recv()
-                    total = total + inbox[step - 1, c].astype(F32)
-                outbox[step, c] = total.astype(BF16)
-                to(step, c).start()
-
-    for g in range(ny // 2):
+    def advance(dy):
+        landed(position(dy, ny))
+        for c in range(chunks):
+            right = way(dy, c, ny) == 1
+            step = reach - dy if right else dy - reach
+            begins = dy == reach or way(dy + 1 if right else dy - 1, c, ny) != way(dy, c, ny)
+            to, outbox, inbox = (
+                (to_right, right_out, right_in) if right else (to_left, left_out, left_in)
+            )
+            total = weighed(dy, c)
+            if not begins:
+                to(step - 1, c).wait_recv()
+                total = total + inbox[step - 1, c].astype(F32)
+            outbox[step, c] = total.astype(BF16)
+            to(step, c).start()
+
+    for g in range(ny // many):
         compute(g)
-        if g:
-            advance(g - 1)
-    for step in range(ny // 2 - 1, reach):
-        advance(step)
+    for dy in sorted(range(1, ny), key=lambda dy: position(dy, ny)):
+        advance(dy)
     landed(ny - 1)
     for c in range(chunks):
         total = weighed(0, c)
         to_right(reach - 1, c).wait_recv()
-        to_left(reach - 2, c).wait_recv()
-        total = total + right_in[reach - 1, c].astype(F32) + left_in[reach - 2, c].astype(F32)
+        to_left(reach - 1, c).wait_recv()
+        total = total + right_in[reach - 1, c].astype(F32) + left_in[reach - 1, c].astype(F32)
         for half in range(2):
             cols = slice(half * HALF + c * wide, half * HALF + (c + 1) * wide)
             out_ref[:, cols] = (
                 stream_ref[:, cols].astype(F32) + total[half * tokens : (half + 1) * tokens, :]
             ).astype(BF16)
     for c in range(chunks):
-        for step in range(reach):
-            to_right(step, c).wait_send()
-        for step in range(reach - 1):
-            to_left(step, c).wait_send()
+        for dy in range(1, ny):
+            if way(dy, c, ny) == 1:
+                to_right(reach - dy, c).wait_send()
+            else:
+                to_left(dy - reach, c).wait_send()
     for p in range(ny):
 
         def finish(k, carry, p=p):
@@ -549,22 +651,20 @@
     slots = count * BLK
     group = 2 * nx * BLK
 
-    stacked = jnp.concatenate([w_gate[0], w_up[0], w_down[0]], axis=0)
-    w_full = lax.all_gather(stacked, "expert", axis=1, tiled=True)
-
     state = (part, HD, HD)
     nz = lax.axis_size("expert")
     depth, shard = proj_weight.shape
     dma = pltpu.SemaphoreType.DMA
-    stream, weighing, incoming = pl.pallas_call(
+    stream, weighing, incoming, *full = pl.pallas_call(
         functools.partial(front_kernel, nx, ny, nz),
         out_shape=[
             jax.ShapeDtypeStruct((token_rows, D), BF16),
             jax.ShapeDtypeStruct((ny, 2 * token_rows, group), BF16),
             jax.ShapeDtypeStruct((slots, HALF), BF16),
+            *[jax.ShapeDtypeStruct((nz, *w_down.shape[1:]), BF16)] * 3,
         ],
-        in_specs=in_vmem(10),
-        out_specs=[*in_vmem(2), pl.BlockSpec(memory_space=pl.ANY)],
+        in_specs=[*in_vmem(10), *[pl.BlockSpec(memory_space=pl.ANY)] * 3],
+        out_specs=[*in_vmem(2), *[pl.BlockSpec(memory_space=pl.ANY)] * 4],
         scratch_shapes=[
             pltpu.VMEM((nx, *state), BF16),
             pltpu.VMEM((nx, *state), BF16),
@@ -574,7 +674,7 @@
             pltpu.VMEM((nx, *state), BF16),
             pltpu.VMEM((tok, width), F32),
             pltpu.VMEM((tok, width), BF16),
-            pltpu.VMEM((nz, depth, shard), BF16),
+            pltpu.VMEM((nz, nx, ny, depth // (nx * ny), shard), BF16),
             pltpu.VMEM((tok, D), F32),
             pltpu.VMEM((token_rows, D), BF16),
             pltpu.VMEM((token_rows, D), BF16),
@@ -584,6 +684,7 @@
             pltpu.VMEM((slots, HALF), BF16),
             *[dma((n,)) for n in (nx, nx, ny, ny, nx, nx, nz, nz, ny, ny, ny, ny, ny, ny, ny, ny, 2)],
             *[dma((n,)) for n in (ny, ny, ny, ny * CHUNKS, ny * CHUNKS, count, count)],
+            *[dma((n,)) for n in (nx, nx, 2 * ny, 2 * ny, 6 * nz, 6 * nz, 3)],
         ],
         compiler_params=pltpu.CompilerParams(
             collective_id=0, has_side_effects=True, vmem_limit_bytes=VMEM_LIMIT
@@ -592,28 +693,28 @@
         name="front",
     )(
         query_proj[0], key_proj[0], value_proj[0], init_state[0], out_gain[None, :], proj_weight,
-        residual[0], moe_gain[None, :], expert_ids[0], gate_weights[0],
+        residual[0], moe_gain[None, :], expert_ids.transpose(2, 0, 1), gate_weights.transpose(2, 0, 1), w_gate[0], w_up[0], w_down[0],
     )
 
     passing = (CHUNKS, 2 * token_rows, HALF // CHUNKS)
     out = pl.pallas_call(
         functools.partial(expert_kernel, nx, ny),
         out_shape=jax.ShapeDtypeStruct((token_rows, D), BF16),
-        in_specs=in_vmem(4),
+        in_specs=in_vmem(6),
         out_specs=pl.BlockSpec(memory_space=pltpu.VMEM),
         scratch_shapes=[
             pltpu.VMEM((slots, HALF), BF16),
             pltpu.VMEM((slots, HALF), BF16),
-            *[pltpu.VMEM((n, *passing), BF16) for n in (ny // 2, ny // 2, ny // 2 - 1, ny // 2 - 1)],
+            *[pltpu.VMEM((n, *passing), BF16) for n in [ny // 2] * 4],
             *[dma((n,)) for n in (count, count)],
-            *[dma((n * CHUNKS,)) for n in (ny // 2, ny // 2, ny // 2 - 1, ny // 2 - 1)],
+            *[dma((n * CHUNKS,)) for n in [ny // 2] * 4],
         ],
         compiler_params=pltpu.CompilerParams(
             collective_id=2, has_side_effects=True, vmem_limit_bytes=VMEM_LIMIT
         ),
         cost_estimate=pl.CostEstimate(flops=5 * 10**9, bytes_accessed=2 * 10**8, transcendentals=0),
         name="experts",
-    )(incoming, w_full, stream, weighing)
+    )(incoming, *full, stream, weighing)
     return out[None]
 
 

time: 175 us -> 154 us (0.88)
  between operations: 13.4 us -> 0.02 us
  Pallas kernels: 155 us -> 152 us
  other arithmetic: 2.28 us -> 0 us
    pallas_call x1, Pallas kernels: 47.9 us -> 45.6 us  [shards(): pl.pallas_call(functools.partial(expert_kernel, nx, ny), out_shape=jax.Sh...]
    concatenate x1 -> x0, other arithmetic: 2.28 us -> none  [shards(): stacked = jnp.concatenate([w_gate[0], w_up[0], w_down[0]], axis=0)]
  transfers between devices with their start and end apart: 1 -> 0, of which waited for: 1 -> 0; matrix products, arithmetic and copies ran while one was open for 1% -> 0% of each run, Pallas kernels for 61% -> 0%
where the time goes in v4:
time: 154 us
  Pallas kernels  152 us (99%)
  local copies, waits for them, and re-layouts  1.67 us (1%)
    pallas_call x1, Pallas kernels, shards(): pl.pallas_call(functools.partial(front_kernel, nx, ny, nz), out_shape=[ja...  106 us
    pallas_call x1, Pallas kernels, shards(): pl.pallas_call(functools.partial(expert_kernel, nx, ny), out_shape=jax.Sh...  45.6 us

profile of v4, /device:TPU:1, one launch (start us, length us, event | category | flops | bytes accessed | tf_op | source)
XLA Modules:
  0.0 153.5 jit_solution(11666178986906471665)
XLA Ops:
  0.0 106.3 %front.1 = (bf16[64,2048]{1,0:T(8,128)(2,1)}, bf16[8,128,128]{2,1,0:T(8,128)(2,1)}, bf16[1024,1024]{1,0:T(8,128)(2,1)}, bf16[8,704,256]{2,1,0:T(8,128)(2,1)}, bf...) custom-call(bf16[128,1024]{1,0:T(8,128)(2,1)} %bitcast.18, bf16[128,1024]{1,0:T(8,128)(2,1)} %bitcast.19, ...), custom_call_target="tpu_custom_call" | custom-call | flops 1000000000 | bytes 300000000 | tf_op jit(solution)/shard_map/front/pallas_call | solution.py:658
  106.3 45.6 %experts.1 = bf16[64,2048]{1,0:T(8,128)(2,1)} custom-call(bf16[1024,1024]{1,0:T(8,128)(2,1)} %get-tuple-element.11.x_ref, bf16[8,704,256]{2,1,0:T(8,128)(2,1)} %get-tuple-element.12.gate_ref, bf16[8,704,256]{2,1,0:T(8,128)(2,1)} %get-tuple-element.13.up_ref, bf16[8,704,256]{2,1,0:T(8,128)(2,1)} %get-tuple-element.14.down_ref, ...), custom_call_target="tpu_custom_call" | custom-call | flops 5000000000 | bytes 200000000 | tf_op jit(solution)/shard_map/experts/pallas_call | solution.py:700
  151.9 1.7 %copy.15 = bf16[1,64,2048]{2,1,0:T(8,128)(2,1)} copy(bf16[1,64,2048]{2,1,0:T(8,128)(2,1)} %bitcast.13) | data formatting | bytes 524288

commit v5 on v4

--- a/solution.py
+++ b/solution.py
@@ -89,13 +89,154 @@
             weighing[i, half * tokens : (half + 1) * tokens, :] = weights[:, i * group : (i + 1) * group]
 
 
-def front_kernel(
+def run_experts(
+    nx, ny, x_ref, gate_ref, up_ref, down_ref, stream_ref, weigh_ref, out_ref, results, returned, right_out, right_in, left_out, left_in,
+    send, recv, right_send, right_recv, left_send, left_recv,
+):
+    s, h, z = lax.axis_index("seq"), lax.axis_index("head"), lax.axis_index("expert")
+    y, x = s // nx, lax.rem(s, nx)
+    across = 2 * nx
+    sub = x * 2 + h
+    reach = ny // 2
+    group = across * BLK
+    tokens = stream_ref.shape[0]
+    many = ny // 2
+    shards_in_half = down_ref.shape[0] // 2
+    chunks, wide = right_out.shape[1], right_out.shape[3]
+
+    def at_sub(k):
+        other = lax.rem(sub + k, across)
+        return (y * nx + other // 2, lax.rem(other, 2), z)
+
+    def at_y(d):
+        return (lax.rem(y + d, ny) * nx + x, h, z)
+
+    def block(p, k, source):
+        slot = p * across + lax.rem(sub + k, across)
+        sem = p * across + k
+        return remote(
+            results.at[rows(slot, BLK), :], returned.at[rows(p * across + source, BLK), :],
+            send.at[sem], recv.at[sem], at_sub(k),
+        )
+
+    def compute(g):
+        span = slice(many * g * group, many * (g + 1) * group)
+        blocks = x_ref[span, :].astype(F32).reshape(many * across, BLK, HALF)
+        low = blocks[:, :CAP].reshape(many * across * CAP, HALF).astype(BF16)
+        high = blocks[:, CAP:].reshape(many * across * CAP, HALF).astype(BF16)
+        acts = []
+        for w_ref in (gate_ref, up_ref):
+            total = None
+            for i, values in enumerate((low, high)):
+                for j in range(shards_in_half):
+                    wide_in = HALF // shards_in_half
+                    term = dot(
+                        values[:, j * wide_in : (j + 1) * wide_in], w_ref[i * shards_in_half + j], ((1,), (1,))
+                    )
+                    total = term if total is None else total + term
+            acts.append(total)
+        gate, up = acts
+        hidden = (gate / (1.0 + jnp.exp(-gate)) * up).astype(BF16)
+        outs = [
+            jnp.concatenate(
+                [dot(hidden, down_ref[i * shards_in_half + j]) for j in range(shards_in_half)], axis=1
+            ).reshape(many * across, CAP, HALF)
+            for i in range(2)
+        ]
+        results[span, :] = (
+            jnp.concatenate(outs, axis=1).reshape(many * across * BLK, HALF).astype(BF16)
+        )
+        for p in range(many * g, many * (g + 1)):
+
+            def begin(k, carry, p=p):
+                block(p, k, sub).start()
+                return carry
+
+            lax.fori_loop(1, across, begin, 0)
+            own = rows(p * across + sub, BLK)
+            returned[own, :] = results[own, :]
+
+    def landed(p):
+        def one(k, carry):
+            block(p, k, lax.rem(sub + across - k, across)).wait_recv()
+            return carry
+
+        lax.fori_loop(1, across, one, 0)
+
+    def weighed(dy, c):
+        p = position(dy, ny)
+        return dot(
+            weigh_ref[(ny - dy) % ny],
+            returned[p * group : (p + 1) * group, c * wide : (c + 1) * wide],
+        )
+
+    def to_right(step, c):
+        sem = step * chunks + c
+        return remote(
+            right_out.at[step, c], right_in.at[step, c], right_send.at[sem], right_recv.at[sem], at_y(1)
+        )
+
+    def to_left(step, c):
+        sem = step * chunks + c
+        return remote(
+            left_out.at[step, c], left_in.at[step, c], left_send.at[sem], left_recv.at[sem], at_y(ny - 1)
+        )
+
+    def advance(dy):
+        landed(position(dy, ny))
+        for c in range(chunks):
+            right = way(dy, c, ny) == 1
+            step = reach - dy if right else dy - reach
+            begins = dy == reach or way(dy + 1 if right else dy - 1, c, ny) != way(dy, c, ny)
+            to, outbox, inbox = (
+                (to_right, right_out, right_in) if right else (to_left, left_out, left_in)
+            )
+            total = weighed(dy, c)
+            if not begins:
+                to(step - 1, c).wait_recv()
+                total = total + inbox[step - 1, c].astype(F32)
+            outbox[step, c] = total.astype(BF16)
+            to(step, c).start()
+
+    for g in range(ny // many):
+        compute(g)
+    for dy in sorted(range(1, ny), key=lambda dy: position(dy, ny)):
+        advance(dy)
+    landed(ny - 1)
+    for c in range(chunks):
+        total = weighed(0, c)
+        to_right(reach - 1, c).wait_recv()
+        to_left(reach - 1, c).wait_recv()
+        total = total + right_in[reach - 1, c].astype(F32) + left_in[reach - 1, c].astype(F32)
+        for half in range(2):
+            cols = slice(half * HALF + c * wide, half * HALF + (c + 1) * wide)
+            out_ref[:, cols] = (
+                stream_ref[:, cols].astype(F32) + total[half * tokens : (half + 1) * tokens, :]
+            ).astype(BF16)
+    for c in range(chunks):
+        for dy in range(1, ny):
+            if way(dy, c, ny) == 1:
+                to_right(reach - dy, c).wait_send()
+            else:
+                to_left(dy - reach, c).wait_send()
+    for p in range(ny):
+
+        def finish(k, carry, p=p):
+            block(p, k, sub).wait_send()
+            return carry
+
+        lax.fori_loop(1, across, finish, 0)
+
+
+def layer_kernel(
     nx, ny, nz, q_ref, k_ref, v_ref, init_ref, out_gain_ref, wo_ref, res_ref, gain_ref, ids_ref, gates_ref, gate_ref, up_ref, down_ref,
-    stream_ref, weigh_ref, incoming_ref, gate_full_ref, up_full_ref, down_full_ref,
+    out_ref,
+    stream_ref, incoming_ref, gate_full_ref, up_full_ref, down_full_ref,
     loc, xin, tot, yin, pre, pin, att, mixed, wo, proj, snd, rcv, own_weighing, weighing, feats, outgoing,
     x_send, x_recv, y_send, y_recv, p_send, p_recv, wz_send, wz_recv, wy_send, wy_recv,
     right_send, right_recv, left_send, left_recv, pass_send, pass_recv, h_sem, g_send, g_recv, own_sem,
     f_send, f_recv, send, recv, bx_send, bx_recv, by_send, by_recv, ring_send, ring_recv, ring_own,
+    *for_experts,
 ):
     s, h, z = lax.axis_index("seq"), lax.axis_index("head"), lax.axis_index("expert")
     y, x = s // nx, lax.rem(s, nx)
@@ -408,7 +549,6 @@
         ring(0, c, ny - 1).start()
     for d in range(1, ny):
         shared[d - 1].wait_recv()
-    weigh_ref[...] = weighing[...]
 
     def block(b, k):
         other = lax.rem(sub + k, across)
@@ -487,151 +627,9 @@
 
         lax.fori_loop(1, across, finish, 0)
 
-
-def expert_kernel(
-    nx, ny, x_ref, gate_ref, up_ref, down_ref, stream_ref, weigh_ref, out_ref, results, returned, right_out, right_in, left_out, left_in,
-    send, recv, right_send, right_recv, left_send, left_recv,
-):
-    s, h, z = lax.axis_index("seq"), lax.axis_index("head"), lax.axis_index("expert")
-    y, x = s // nx, lax.rem(s, nx)
-    across = 2 * nx
-    sub = x * 2 + h
-    reach = ny // 2
-    group = across * BLK
-    tokens = stream_ref.shape[0]
-    many = ny // 2
-    shards_in_half = down_ref.shape[0] // 2
-    chunks, wide = right_out.shape[1], right_out.shape[3]
-
-    def at_sub(k):
-        other = lax.rem(sub + k, across)
-        return (y * nx + other // 2, lax.rem(other, 2), z)
-
-    def at_y(d):
-        return (lax.rem(y + d, ny) * nx + x, h, z)
-
-    barrier = pltpu.get_barrier_semaphore()
-    peers = [at_y(1), at_y(ny - 1), *[at_sub(k) for k in range(1, across)]]
-    for peer in peers:
-        pl.semaphore_signal(barrier, inc=1, device_id=peer, device_id_type=MESH)
-
-    def block(p, k, source):
-        slot = p * across + lax.rem(sub + k, across)
-        sem = p * across + k
-        return remote(
-            results.at[rows(slot, BLK), :], returned.at[rows(p * across + source, BLK), :],
-            send.at[sem], recv.at[sem], at_sub(k),
-        )
-
-    def compute(g):
-        span = slice(many * g * group, many * (g + 1) * group)
-        blocks = x_ref[span, :].astype(F32).reshape(many * across, BLK, HALF)
-        low = blocks[:, :CAP].reshape(many * across * CAP, HALF).astype(BF16)
-        high = blocks[:, CAP:].reshape(many * across * CAP, HALF).astype(BF16)
-        acts = []
-        for w_ref in (gate_ref, up_ref):
-            total = None
-            for i, values in enumerate((low, high)):
-                for j in range(shards_in_half):
-                    wide_in = HALF // shards_in_half
-                    term = dot(
-                        values[:, j * wide_in : (j + 1) * wide_in], w_ref[i * shards_in_half + j], ((1,), (1,))
-                    )
-                    total = term if total is None else total + term
-            acts.append(total)
-        gate, up = acts
-        hidden = (gate / (1.0 + jnp.exp(-gate)) * up).astype(BF16)
-        outs = [
-            jnp.concatenate(
-                [dot(hidden, down_ref[i * shards_in_half + j]) for j in range(shards_in_half)], axis=1
-            ).reshape(many * across, CAP, HALF)
-            for i in range(2)
-        ]
-        results[span, :] = (
-            jnp.concatenate(outs, axis=1).reshape(many * across * BLK, HALF).astype(BF16)
-        )
-        if g == 0:
-            pl.semaphore_wait(barrier, len(peers))
-        for p in range(many * g, many * (g + 1)):
-
-            def begin(k, carry, p=p):
-                block(p, k, sub).start()
-                return carry
-
-            lax.fori_loop(1, across, begin, 0)
-            own = rows(p * across + sub, BLK)
-            returned[own, :] = results[own, :]
-
-    def landed(p):
-        def one(k, carry):
-            block(p, k, lax.rem(sub + across - k, across)).wait_recv()
-            return carry
-
-        lax.fori_loop(1, across, one, 0)
-
-    def weighed(dy, c):
-        p = position(dy, ny)
-        return dot(
-            weigh_ref[(ny - dy) % ny],
-            returned[p * group : (p + 1) * group, c * wide : (c + 1) * wide],
-        )
-
-    def to_right(step, c):
-        sem = step * chunks + c
-        return remote(
-            right_out.at[step, c], right_in.at[step, c], right_send.at[sem], right_recv.at[sem], at_y(1)
-        )
-
-    def to_left(step, c):
-        sem = step * chunks + c
-        return remote(
-            left_out.at[step, c], left_in.at[step, c], left_send.at[sem], left_recv.at[sem], at_y(ny - 1)
-        )
-
-    def advance(dy):
-        landed(position(dy, ny))
-        for c in range(chunks):
-            right = way(dy, c, ny) == 1
-            step = reach - dy if right else dy - reach
-            begins = dy == reach or way(dy + 1 if right else dy - 1, c, ny) != way(dy, c, ny)
-            to, outbox, inbox = (
-                (to_right, right_out, right_in) if right else (to_left, left_out, left_in)
-            )
-            total = weighed(dy, c)
-            if not begins:
-                to(step - 1, c).wait_recv()
-                total = total + inbox[step - 1, c].astype(F32)
-            outbox[step, c] = total.astype(BF16)
-            to(step, c).start()
-
-    for g in range(ny // many):
-        compute(g)
-    for dy in sorted(range(1, ny), key=lambda dy: position(dy, ny)):
-        advance(dy)
-    landed(ny - 1)
-    for c in range(chunks):
-        total = weighed(0, c)
-        to_right(reach - 1, c).wait_recv()
-        to_left(reach - 1, c).wait_recv()
-        total = total + right_in[reach - 1, c].astype(F32) + left_in[reach - 1, c].astype(F32)
-        for half in range(2):
-            cols = slice(half * HALF + c * wide, half * HALF + (c + 1) * wide)
-            out_ref[:, cols] = (
-                stream_ref[:, cols].astype(F32) + total[half * tokens : (half + 1) * tokens, :]
-            ).astype(BF16)
-    for c in range(chunks):
-        for dy in range(1, ny):
-            if way(dy, c, ny) == 1:
-                to_right(reach - dy, c).wait_send()
-            else:
-                to_left(dy - reach, c).wait_send()
-    for p in range(ny):
-
-        def finish(k, carry, p=p):
-            block(p, k, sub).wait_send()
-            return carry
-
-        lax.fori_loop(1, across, finish, 0)
+    run_experts(
+        nx, ny, incoming_ref, gate_full_ref, up_full_ref, down_full_ref, stream_ref, weighing, out_ref, *for_experts
+    )
 
 
 def in_vmem(n):
@@ -655,17 +653,16 @@
     nz = lax.axis_size("expert")
     depth, shard = proj_weight.shape
     dma = pltpu.SemaphoreType.DMA
-    stream, weighing, incoming, *full = pl.pallas_call(
-        functools.partial(front_kernel, nx, ny, nz),
-        out_shape=[
-            jax.ShapeDtypeStruct((token_rows, D), BF16),
-            jax.ShapeDtypeStruct((ny, 2 * token_rows, group), BF16),
-            jax.ShapeDtypeStruct((slots, HALF), BF16),
-            *[jax.ShapeDtypeStruct((nz, *w_down.shape[1:]), BF16)] * 3,
-        ],
+    passing = (CHUNKS, 2 * token_rows, HALF // CHUNKS)
+    out = pl.pallas_call(
+        functools.partial(layer_kernel, nx, ny, nz),
+        out_shape=jax.ShapeDtypeStruct((token_rows, D), BF16),
         in_specs=[*in_vmem(10), *[pl.BlockSpec(memory_space=pl.ANY)] * 3],
-        out_specs=[*in_vmem(2), *[pl.BlockSpec(memory_space=pl.ANY)] * 4],
+        out_specs=pl.BlockSpec(memory_space=pltpu.VMEM),
         scratch_shapes=[
+            pltpu.VMEM((token_rows, D), BF16),
+            pltpu.VMEM((slots, HALF), BF16),
+            *[pltpu.VMEM((nz, *w_down.shape[1:]), BF16)] * 3,
             pltpu.VMEM((nx, *state), BF16),
             pltpu.VMEM((nx, *state), BF16),
             pltpu.VMEM(state, BF16),
@@ -685,24 +682,6 @@
             *[dma((n,)) for n in (nx, nx, ny, ny, nx, nx, nz, nz, ny, ny, ny, ny, ny, ny, ny, ny, 2)],
             *[dma((n,)) for n in (ny, ny, ny, ny * CHUNKS, ny * CHUNKS, count, count)],
             *[dma((n,)) for n in (nx, nx, 2 * ny, 2 * ny, 6 * nz, 6 * nz, 3)],
-        ],
-        compiler_params=pltpu.CompilerParams(
-            collective_id=0, has_side_effects=True, vmem_limit_bytes=VMEM_LIMIT
-        ),
-        cost_estimate=pl.CostEstimate(flops=10**9, bytes_accessed=3 * 10**8, transcendentals=0),
-        name="front",
-    )(
-        query_proj[0], key_proj[0], value_proj[0], init_state[0], out_gain[None, :], proj_weight,
-        residual[0], moe_gain[None, :], expert_ids.transpose(2, 0, 1), gate_weights.transpose(2, 0, 1), w_gate[0], w_up[0], w_down[0],
-    )
-
-    passing = (CHUNKS, 2 * token_rows, HALF // CHUNKS)
-    out = pl.pallas_call(
-        functools.partial(expert_kernel, nx, ny),
-        out_shape=jax.ShapeDtypeStruct((token_rows, D), BF16),
-        in_specs=in_vmem(6),
-        out_specs=pl.BlockSpec(memory_space=pltpu.VMEM),
-        scratch_shapes=[
             pltpu.VMEM((slots, HALF), BF16),
             pltpu.VMEM((slots, HALF), BF16),
             *[pltpu.VMEM((n, *passing), BF16) for n in [ny // 2] * 4],
@@ -710,11 +689,14 @@
             *[dma((n * CHUNKS,)) for n in [ny // 2] * 4],
         ],
         compiler_params=pltpu.CompilerParams(
-            collective_id=2, has_side_effects=True, vmem_limit_bytes=VMEM_LIMIT
+            collective_id=0, has_side_effects=True, vmem_limit_bytes=VMEM_LIMIT
         ),
-        cost_estimate=pl.CostEstimate(flops=5 * 10**9, bytes_accessed=2 * 10**8, transcendentals=0),
-        name="experts",
-    )(incoming, *full, stream, weighing)
+        cost_estimate=pl.CostEstimate(flops=10**9, bytes_accessed=3 * 10**8, transcendentals=0),
+        name="layer",
+    )(
+        query_proj[0], key_proj[0], value_proj[0], init_state[0], out_gain[None, :], proj_weight,
+        residual[0], moe_gain[None, :], expert_ids.transpose(2, 0, 1), gate_weights.transpose(2, 0, 1), w_gate[0], w_up[0], w_down[0],
+    )
     return out[None]
 
 

time: 154 us -> 148 us (0.961)
  Pallas kernels: 152 us -> 146 us
    pallas_call x2 -> x1, Pallas kernels: 152 us -> 146 us  [shards(): pl.pallas_call(functools.partial(layer_kernel, nx, ny, nz), out_shape=jax...]
where the time goes in v5:
time: 148 us
  Pallas kernels  146 us (99%)
  local copies, waits for them, and re-layouts  1.67 us (1%)
    pallas_call x1, Pallas kernels, shards(): pl.pallas_call(functools.partial(layer_kernel, nx, ny, nz), out_shape=jax...  146 us

profile of v5, /device:TPU:1, one launch (start us, length us, event | category | flops | bytes accessed | tf_op | source)
XLA Modules:
  0.0 147.8 jit_solution(6162929977154440944)
XLA Ops:
  0.0 146.1 %layer.1 = bf16[64,2048]{1,0:T(8,128)(2,1)} custom-call(bf16[128,1024]{1,0:T(8,128)(2,1)} %bitcast.18, bf16[128,1024]{1,0:T(8,128)(2,1)} %bitcast.19, bf16[128,1024]{1,0:T(8,128)(2,1)} %bitcast.20, f32[8,128,128]{2,1,0:T(8,128)} %bitcast.14, f32[1,1024]{1,0:T(1,128)} %bitcast.23, bf16[1024,256]{1,0:T(8,128)(2,1)} %wo_ref.1, bf16[64,2048]{1,0:T(8,128)(2,1)} %bitcast.21, ...), custom_call_target="tpu_custom_call" | custom-call | flops 1000000000 | bytes 300000000 | tf_op jit(solution)/shard_map/layer/pallas_call | solution.py:657
  146.1 1.7 %copy.15 = bf16[1,64,2048]{2,1,0:T(8,128)(2,1)} copy(bf16[1,64,2048]{2,1,0:T(8,128)(2,1)} %bitcast.13) | data formatting | bytes 524288

commit v6 on v5

--- a/solution.py
+++ b/solution.py
@@ -90,8 +90,8 @@
 
 
 def run_experts(
-    nx, ny, x_ref, gate_ref, up_ref, down_ref, stream_ref, weigh_ref, out_ref, results, returned, right_out, right_in, left_out, left_in,
-    send, recv, right_send, right_recv, left_send, left_recv,
+    nx, ny, nz, last, x_ref, gate_ref, up_ref, down_ref, stream_ref, weigh_ref, out_ref, results, returned, right_out, right_in, left_out, left_in,
+    send, recv, right_send, right_recv, left_send, left_recv, spread_in, acts,
 ):
     s, h, z = lax.axis_index("seq"), lax.axis_index("head"), lax.axis_index("expert")
     y, x = s // nx, lax.rem(s, nx)
@@ -119,23 +119,35 @@
             send.at[sem], recv.at[sem], at_sub(k),
         )
 
+    group_rows = many * across * CAP
+
+    def partial(g):
+        span = slice(many * g * group, many * (g + 1) * group)
+        mine = slice(g * group_rows, (g + 1) * group_rows)
+        blocks = x_ref[span, :].astype(F32).reshape(many * across, BLK, HALF)
+        wide_in = HALF // shards_in_half
+        for i in range(2):
+            values = blocks[:, i * CAP : (i + 1) * CAP].reshape(group_rows, HALF).astype(BF16)
+            for j in range(shards_in_half):
+                spread_in[i * shards_in_half + j, mine, :] = values[:, j * wide_in : (j + 1) * wide_in]
+        for m, w_ref in enumerate((gate_ref, up_ref)):
+            total = None
+            for b in range(nz):
+                if b == nz // 2:
+                    continue
+                owner = lax.rem(z + nz - b, nz)
+                term = dot(spread_in[owner, mine, :], w_ref[owner], ((1,), (1,)))
+                total = term if total is None else total + term
+            acts[m, mine, :] = total
+
     def compute(g):
         span = slice(many * g * group, many * (g + 1) * group)
-        blocks = x_ref[span, :].astype(F32).reshape(many * across, BLK, HALF)
-        low = blocks[:, :CAP].reshape(many * across * CAP, HALF).astype(BF16)
-        high = blocks[:, CAP:].reshape(many * across * CAP, HALF).astype(BF16)
-        acts = []
-        for w_ref in (gate_ref, up_ref):
-            total = None
-            for i, values in enumerate((low, high)):
-                for j in range(shards_in_half):
-                    wide_in = HALF // shards_in_half
-                    term = dot(
-                        values[:, j * wide_in : (j + 1) * wide_in], w_ref[i * shards_in_half + j], ((1,), (1,))
-                    )
-                    total = term if total is None else total + term
-            acts.append(total)
-        gate, up = acts
+        mine = slice(g * group_rows, (g + 1) * group_rows)
+        owner = lax.rem(z + nz // 2, nz)
+        gate, up = (
+            acts[m, mine, :] + dot(spread_in[owner, mine, :], w_ref[owner], ((1,), (1,)))
+            for m, w_ref in enumerate((gate_ref, up_ref))
+        )
         hidden = (gate / (1.0 + jnp.exp(-gate)) * up).astype(BF16)
         outs = [
             jnp.concatenate(
@@ -198,6 +210,9 @@
             outbox[step, c] = total.astype(BF16)
             to(step, c).start()
 
+    for g in range(ny // many):
+        partial(g)
+    last()
     for g in range(ny // many):
         compute(g)
     for dy in sorted(range(1, ny), key=lambda dy: position(dy, ny)):
@@ -318,9 +333,8 @@
 
     for d in range(1, nz):
         fetch(d, z).start()
-    for i in range(pieces):
-        for step in (1, nz - 1):
-            piece(0, i, step).start()
+    for step in (1, nz - 1):
+        piece(0, 0, step).start()
     kept = [
         pltpu.make_async_copy(share, full.at[z], ring_own.at[i])
         for i, (share, full) in enumerate(zip(shares, fulls, strict=True))
@@ -408,19 +422,23 @@
     for d in range(1, nx):
         side(d).start()
     spread(0)
-
-    with jax.named_scope("inner"):
-        positions = q_ref.shape[0]
-        causal = lax.broadcasted_iota(jnp.int32, (positions, positions), 0) >= lax.broadcasted_iota(
-            jnp.int32, (positions, positions), 1
-        )
-        for i in range(heads):
+    for i in range(1, pieces):
+        for step in (1, nz - 1):
+            piece(0, i, step).start()
+
+    positions = q_ref.shape[0]
+    causal = lax.broadcasted_iota(jnp.int32, (positions, positions), 0) >= lax.broadcasted_iota(
+        jnp.int32, (positions, positions), 1
+    )
+
+    def inner(begin, end):
+        for i in range(begin, end):
             cols = slice(i * HD, (i + 1) * HD)
             scores = dot(q_ref[:, cols], k_ref[:, cols], ((1,), (1,)))
             scores = jnp.where(causal, scores, 0.0).astype(BF16)
             att[:, cols] = dot(scores, v_ref[:, cols])
-    with jax.named_scope("placing"):
-        place(ids_ref, gates_ref, own_weighing)
+
+    inner(0, heads // 2)
     with jax.named_scope("relay_1"):
         for d in range(1, nx):
             side_came(d).wait_recv()
@@ -430,9 +448,11 @@
         relay_y(1)
         relay_y(ny - 1)
         relay_x(0)
+        inner(heads // 2, heads)
         relay_row(1)
         relay_row(ny - 1)
-        relay_ring(1, 0)
+        relay_y(2)
+        relay_y(ny - 2)
 
     before = jnp.zeros(tot.shape, F32)
     with jax.named_scope("states_y"):
@@ -454,17 +474,21 @@
     pin[0] = pre[0]
     with jax.named_scope("relay_2"):
         for step in range(2, reach):
-            relay_y(step)
-            relay_y(ny - step)
+            if step > 2:
+                relay_y(step)
+                relay_y(ny - step)
             relay_row(step)
             relay_row(ny - step)
             relay_x(step - 1)
             relay_x(ny - step + 1)
+            if step == 2:
+                relay_ring(1, 0)
         relay_y(reach)
         relay_row(reach)
         relay_x(reach - 1)
         relay_x(reach + 1)
         relay_ring(1, 1)
+    place(ids_ref, gates_ref, own_weighing)
     weighing[0] = own_weighing[y]
     shared = [
         remote(
@@ -496,12 +520,18 @@
                 along_x(b, 2, pass_send, pass_recv, nx - 1).wait_recv()
 
     relay_ring(2, 0)
-    with jax.named_scope("project"):
-        for c in range(nz):
-            proj[:, c * width : (c + 1) * width] = dot(mixed[...], wo[c].reshape(nx * ny * depth, width))
-    snd[...] = proj[rows(1 - h, tokens), :].astype(BF16)
-    half = remote(snd, rcv, h_sem.at[0], h_sem.at[1], (s, 1 - h, z))
-    half.start()
+    halves = []
+    for j in range(2):
+        for c in range(j * nz // 2, (j + 1) * nz // 2):
+            proj[:, c * width : (c + 1) * width] = dot(
+                mixed[...], wo[c].reshape(nx * ny * depth, width)
+            )
+        cols = slice(j * HALF, (j + 1) * HALF)
+        snd[j] = proj[rows(1 - h, tokens), cols].astype(BF16)
+        halves.append(
+            remote(snd.at[j], rcv.at[j], h_sem.at[j], h_sem.at[2 + j], (s, 1 - h, z))
+        )
+        halves[j].start()
     relay_ring(2, 1)
     for copy in first + second + third:
         copy.wait_send()
@@ -523,10 +553,11 @@
                 row_came(b, c).wait_send()
     for d in range(1, nx):
         side(d).wait_send()
-    with jax.named_scope("other_half"):
+    for half in halves:
         half.wait_recv()
+    other = jnp.concatenate([rcv[0], rcv[1]], axis=1).astype(F32)
     stream = (
-        res_ref[...].astype(F32) + (proj[rows(h, tokens), :] + rcv[...].astype(F32))
+        res_ref[...].astype(F32) + (proj[rows(h, tokens), :] + other)
     ).astype(BF16)
     stream_ref[...] = stream
     stream_f = stream.astype(F32)
@@ -603,20 +634,16 @@
         lax.fori_loop(1, across, begin, 0)
         keep(b).start()
 
-    half.wait_send()
+    for half in halves:
+        half.wait_send()
     for copy in shared:
         copy.wait_send()
     for b in range(1, ny):
         for c in range(chunks):
             step = way(b, c, ny)
             ring((b - step) % ny, c, step).wait_send()
-    for later in range(2):
-        relay_ring(nz // 2, later)
     for copy in kept:
         copy.wait()
-    for b in range(1, nz):
-        for i in range(pieces):
-            piece_came(b, i).wait_send()
     for b in around:
         keep(b).wait()
 
@@ -627,9 +654,16 @@
 
         lax.fori_loop(1, across, finish, 0)
 
+    def last():
+        for later in range(2):
+            relay_ring(nz // 2, later)
+
     run_experts(
-        nx, ny, incoming_ref, gate_full_ref, up_full_ref, down_full_ref, stream_ref, weighing, out_ref, *for_experts
+        nx, ny, nz, last, incoming_ref, gate_full_ref, up_full_ref, down_full_ref, stream_ref, weighing, out_ref, *for_experts
     )
+    for b in range(1, nz):
+        for i in range(pieces):
+            piece_came(b, i).wait_send()
 
 
 def in_vmem(n):
@@ -673,13 +707,13 @@
             pltpu.VMEM((tok, width), BF16),
             pltpu.VMEM((nz, nx, ny, depth // (nx * ny), shard), BF16),
             pltpu.VMEM((tok, D), F32),
-            pltpu.VMEM((token_rows, D), BF16),
-            pltpu.VMEM((token_rows, D), BF16),
+            pltpu.VMEM((2, token_rows, HALF), BF16),
+            pltpu.VMEM((2, token_rows, HALF), BF16),
             pltpu.VMEM((ny, 2 * token_rows, group), BF16),
             pltpu.VMEM((ny, 2 * token_rows, group), BF16),
             pltpu.VMEM((ny, CHUNKS, 2 * token_rows, HALF // CHUNKS), BF16),
             pltpu.VMEM((slots, HALF), BF16),
-            *[dma((n,)) for n in (nx, nx, ny, ny, nx, nx, nz, nz, ny, ny, ny, ny, ny, ny, ny, ny, 2)],
+            *[dma((n,)) for n in (nx, nx, ny, ny, nx, nx, nz, nz, ny, ny, ny, ny, ny, ny, ny, ny, 4)],
             *[dma((n,)) for n in (ny, ny, ny, ny * CHUNKS, ny * CHUNKS, count, count)],
             *[dma((n,)) for n in (nx, nx, 2 * ny, 2 * ny, 6 * nz, 6 * nz, 3)],
             pltpu.VMEM((slots, HALF), BF16),
@@ -687,6 +721,8 @@
             *[pltpu.VMEM((n, *passing), BF16) for n in [ny // 2] * 4],
             *[dma((n,)) for n in (count, count)],
             *[dma((n * CHUNKS,)) for n in [ny // 2] * 4],
+            pltpu.VMEM((nz, count * CAP, D // nz), BF16),
+            pltpu.VMEM((2, count * CAP, w_down.shape[1]), F32),
         ],
         compiler_params=pltpu.CompilerParams(
             collective_id=0, has_side_effects=True, vmem_limit_bytes=VMEM_LIMIT

time: 148 us -> 147 us (level)
  no operation moved by 1% of the time
where the time goes in v6:
time: 147 us
  Pallas kernels  145 us (99%)
  local copies, waits for them, and re-layouts  1.67 us (1%)
    pallas_call x1, Pallas kernels, shards(): pl.pallas_call(functools.partial(layer_kernel, nx, ny, nz), out_shape=jax...  145 us

profile of v6, /device:TPU:1, one launch (start us, length us, event | category | flops | bytes accessed | tf_op | source)
XLA Modules:
  0.0 146.7 jit_solution(12135033189292987018)
XLA Ops:
  0.0 145.1 %layer.1 = bf16[64,2048]{1,0:T(8,128)(2,1)} custom-call(bf16[128,1024]{1,0:T(8,128)(2,1)} %bitcast.18, bf16[128,1024]{1,0:T(8,128)(2,1)} %bitcast.19, bf16[128,1024]{1,0:T(8,128)(2,1)} %bitcast.20, f32[8,128,128]{2,1,0:T(8,128)} %bitcast.14, f32[1,1024]{1,0:T(1,128)} %bitcast.23, bf16[1024,256]{1,0:T(8,128)(2,1)} %wo_ref.1, bf16[64,2048]{1,0:T(8,128)(2,1)} %bitcast.21, ...), custom_call_target="tpu_custom_call" | custom-call | flops 1000000000 | bytes 300000000 | tf_op jit(solution)/shard_map/layer/pallas_call | solution.py:691
  145.1 1.7 %copy.15 = bf16[1,64,2048]{2,1,0:T(8,128)(2,1)} copy(bf16[1,64,2048]{2,1,0:T(8,128)(2,1)} %bitcast.13) | data formatting | bytes 524288
